TPU v7x, 256 devices: a whole 4x4x8 slice. The times are simulated.
256 devices in a mesh: win: 8 (over y, z_lo), rcv: 32 (over x, z_hi, core).
Axes of the slice: x: 4, y: 4, z: 8 (z_hi: 4, z_lo: 2; z = z_hi * 2 + z_lo), core: 2. Of those that a mesh axis runs over, the one named last changes fastest.
Arguments:
- source_spectra: bfloat16 [256, 4096, 1024], P('win', 'rcv'), may hold values from -6 to 6
- receiver_spectra: bfloat16 [256, 512, 1024], P('win', 'rcv'), may hold values from -6 to 6
- source_block: int32 [1], replicated, may hold values from 0 to 31
- bad_channels: int32 [64], replicated, may hold values from 0 to 511
Outputs:
- correlations: float32 [128, 512, 1024], P('win', 'rcv')
Inputs may be any that keep to these rules, and one draw needn't show every extreme that they name: `source_block`: the rcv index of the device that holds the block. `bad_channels`: repeats may occur.
All inputs are finite; a program needn't handle non-finite values.
Results may differ from a plain program's by a relative error of at most 0.0036.
Values may be sent and summed in bfloat16 or wider, within the bound.
No kernel may reach another device: no remote copies, remote signals or barrier semaphores. Data moves between devices by JAX's collectives and lax.ppermute only.
A program may use at most 128 MiB of HBM per device.

v0:
```python
import functools
import math

import jax
import jax.numpy as jnp
import numpy as np
from jax import lax
from jax.experimental import pallas as pl
from jax.experimental.pallas import tpu as pltpu
from jax.sharding import Mesh
from jax.sharding import PartitionSpec as P

AXES = ("y", "zl", "x", "zh", "core")
SIZES = (4, 2, 4, 4, 2)
LAGS = 1024
HALF = 512
WINDOWS = 256
VMEM = 60 * 1024 * 1024
BF16 = jnp.bfloat16
F32 = jnp.float32


def whiten_parts(re, im, keep=None):
    power = re * re + im * im
    level = jnp.mean(power, axis=-1, keepdims=True)
    factor = lax.rsqrt(power + 0.1 * level + 1e-06)
    if keep is not None:
        factor = factor * keep
    return re * factor, im * factor


def source_kernel(place, src_ref, far_low, far_high, up, down, own, held):
    x = place[0]
    step, steps = pl.program_id(0), pl.num_programs(0)
    data = src_ref[...].astype(F32)
    re, im = (
        jnp.concatenate(
            [part[:, w * 16 + k * 8 : w * 16 + k * 8 + 8] for k in range(2) for w in range(8)],
            axis=1,
        )
        for part in whiten_parts(data[..., :HALF], data[..., HALF:])
    )
    for q in range(4):
        lanes = slice(q * 128, q * 128 + 128)
        held[q, :, :, :128] = re[..., lanes].astype(BF16)
        held[q, :, :, 128:] = im[..., lanes].astype(BF16)
    own[...] = held[x]
    up[...] = held[lax.rem(x + 1, 4)]
    down[...] = held[lax.rem(x + 3, 4)]

    @pl.when(step < steps // 2)
    def _():
        far_low[...] = held[lax.rem(x + 2, 4)]

    @pl.when(step >= steps // 2)
    def _():
        far_high[...] = held[lax.rem(x + 2, 4)]


def source_pieces(src, place):
    windows, sources, _ = src.shape
    block = 4
    steps = windows // block
    part = jax.ShapeDtypeStruct((windows // 2, sources, 256), BF16)
    piece = jax.ShapeDtypeStruct((windows, sources, 256), BF16)
    shape = (block, sources, 256)
    low = pl.BlockSpec(shape, lambda i, p: (jnp.minimum(i, steps // 2 - 1), 0, 0))
    high = pl.BlockSpec(shape, lambda i, p: (jnp.maximum(i - steps // 2, 0), 0, 0))
    plain = pl.BlockSpec(shape, lambda i, p: (i, 0, 0))
    return pl.pallas_call(
        source_kernel,
        out_shape=[part] * 2 + [piece] * 3,
        grid_spec=pltpu.PrefetchScalarGridSpec(
            num_scalar_prefetch=1,
            grid=(steps,),
            in_specs=[pl.BlockSpec((block, sources, LAGS), lambda i, p: (i, 0, 0))],
            out_specs=[low, high] + [plain] * 3,
            scratch_shapes=[pltpu.VMEM((4,) + shape, BF16)],
        ),
        compiler_params=pltpu.CompilerParams(vmem_limit_bytes=VMEM),
        cost_estimate=pl.CostEstimate(
            flops=40_000_000, bytes_accessed=16 * 2**20, transcendentals=2_000_000
        ),
    )(place, src)


def turn_pair(*parts):
    tall = jnp.concatenate(parts, axis=0).T
    low = lax.broadcasted_iota(jnp.int32, (64, 128), 1) < 64
    top, bottom = tall[:64], tall[64:]
    return (
        jnp.where(low, top, pltpu.roll(bottom, 64, axis=1)),
        jnp.where(low, pltpu.roll(top, 64, axis=1), bottom),
    )


def receiver_kernel(place, bad, rcv_ref, out_ref, held, turned):
    windows, chans, _ = rcv_ref.shape
    ids = place[1] * chans + lax.broadcasted_iota(jnp.int32, (chans, 128), 0)
    faulty = ids < 0
    for i in range(bad.shape[0]):
        faulty = faulty | (ids == bad[i])
    keep = jnp.where(faulty, 0.0, 1.0).astype(F32)[None, :, :1]
    group = 4

    @pl.loop(0, windows // group)
    def _(j):
        data = rcv_ref[pl.ds(j * group, group)].astype(F32)
        parts = whiten_parts(data[..., :HALF], data[..., HALF:], keep)
        rows = pl.ds(pl.multiple_of(j * group * chans, group * chans), group * chans)
        for q in range(4):
            for i in range(2):
                lanes = parts[i][..., q * 128 : q * 128 + 128]
                held[2 * q + i, rows, :] = lanes.reshape(group * chans, 128)

    @pl.loop(0, 4)
    def _(q):
        for c in range(0, chans, 2):
            pair = turn_pair(
                *(
                    held[2 * q + part, pl.ds(c + i, windows, stride=chans), :]
                    for i in range(2)
                    for part in range(2)
                )
            )
            for i in range(2):
                turned[pl.ds(q * 64 * chans + c + i, 64, stride=chans), :] = pair[i]

    @pl.loop(0, 8)
    def _(j):
        rows = turned[pl.ds(pl.multiple_of(j * 32 * chans, 32 * chans), 32 * chans), :]
        out_ref[pl.ds(j * 32, 32)] = rows.reshape(32, chans, 128).astype(BF16)


def receiver_blocks(rcv, place, bad):
    windows, chans, _ = rcv.shape
    return pl.pallas_call(
        receiver_kernel,
        out_shape=jax.ShapeDtypeStruct((256, chans, 128), BF16),
        grid_spec=pltpu.PrefetchScalarGridSpec(
            num_scalar_prefetch=2,
            grid=(1,),
            in_specs=[pl.BlockSpec(rcv.shape, lambda i, p, b: (0, 0, 0))],
            out_specs=pl.BlockSpec((256, chans, 128), lambda i, p, b: (0, 0, 0)),
            scratch_shapes=[
                pltpu.VMEM((8, windows * chans, 128), F32),
                pltpu.VMEM((256 * chans, 128), F32),
            ],
        ),
        compiler_params=pltpu.CompilerParams(vmem_limit_bytes=VMEM),
        cost_estimate=pl.CostEstimate(
            flops=20_000_000, bytes_accessed=2 * 2**20, transcendentals=300_000
        ),
    )(place, bad, rcv)


def take(away, pieces, core, target, sem):
    windows = target.shape[0]
    far_low, far_high, up, down, own = (ref.at[:, pl.ds(core * 64, 64)] for ref in pieces)

    def fetch(pairs):
        copies = [pltpu.make_async_copy(a, b, sem.at[i]) for i, (a, b) in enumerate(pairs)]
        for copy in copies:
            copy.start()
        for copy in copies:
            copy.wait()

    mid = windows // 2
    low, high = target.at[pl.ds(0, mid)], target.at[pl.ds(mid, mid)]
    for distance, pairs in (
        (0, [(own, target)]),
        (1, [(up, target)]),
        (2, [(far_low, low), (far_high, high)]),
        (3, [(down, target)]),
    ):
        pl.when(away == distance)(functools.partial(fetch, pairs))


def share_kernel(core, place, *refs):
    take(place[3], refs[:5], core, refs[5], refs[6])


def share(core, place, pieces):
    windows = pieces[-1].shape[0]
    return pl.pallas_call(
        functools.partial(share_kernel, core),
        out_shape=jax.ShapeDtypeStruct((windows, 64, 256), BF16),
        grid_spec=pltpu.PrefetchScalarGridSpec(
            num_scalar_prefetch=1,
            grid=(1,),
            in_specs=[pl.BlockSpec(memory_space=pl.ANY)] * 5,
            out_specs=pl.BlockSpec((windows, 64, 256), lambda i, p: (0, 0, 0)),
            scratch_shapes=[pltpu.SemaphoreType.DMA((2,))],
        ),
        compiler_params=pltpu.CompilerParams(vmem_limit_bytes=VMEM),
    )(place, *pieces)


def turn_kernel(holder_core, place, *refs):
    shared, out_ref, piece, held, turned, sem = refs[5:]
    windows = piece.shape[0]

    @pl.when(place[2] == holder_core)
    def _():
        take(place[3], refs[:5], holder_core, piece, sem)

    @pl.when(place[2] != holder_core)
    def _():
        copy = pltpu.make_async_copy(shared, piece, sem.at[0])
        copy.start()
        copy.wait()

    @pl.loop(0, windows // 4)
    def _(j):
        rows = pl.ds(pl.multiple_of(j * 256, 256), 256)
        for part in range(2):
            lanes = piece[pl.ds(j * 4, 4), :, part * 128 : part * 128 + 128]
            held[part, rows, :] = lanes.astype(F32).reshape(256, 128)

    @pl.loop(0, 8)
    def _(s):
        for w in range(0, 8, 2):
            pair = turn_pair(
                *(
                    held[part, pl.ds(w * 8 + i * 8 + s, windows, stride=64), :]
                    for i in range(2)
                    for part in range(2)
                )
            )
            for i in range(2):
                turned[pl.ds(s * 8 + w + i, 64, stride=64), :] = pair[i]

    @pl.loop(0, 8)
    def _(j):
        rows = turned[pl.ds(pl.multiple_of(j * 512, 512), 512), :]
        out_ref[pl.ds(j * 8, 8)] = rows.reshape(8, 64, 128).astype(BF16)


def turn_source(holder_core, place, pieces, shared):
    windows = pieces[-1].shape[0]
    return pl.pallas_call(
        functools.partial(turn_kernel, holder_core),
        out_shape=jax.ShapeDtypeStruct((64, 64, 128), BF16),
        grid_spec=pltpu.PrefetchScalarGridSpec(
            num_scalar_prefetch=1,
            grid=(1,),
            in_specs=[pl.BlockSpec(memory_space=pl.ANY)] * 6,
            out_specs=pl.BlockSpec((64, 64, 128), lambda i, p: (0, 0, 0)),
            scratch_shapes=[
                pltpu.VMEM((windows, 64, 256), BF16),
                pltpu.VMEM((2, windows * 64, 128), F32),
                pltpu.VMEM((64 * 64, 128), F32),
                pltpu.SemaphoreType.DMA((2,)),
            ],
        ),
        compiler_params=pltpu.CompilerParams(vmem_limit_bytes=VMEM),
    )(place, *pieces, shared)


def cross_kernel(place, src_ref, rcv_ref, out_ref, acc):
    row = lax.broadcasted_iota(jnp.int32, (512, 128), 0)
    col = lax.broadcasted_iota(jnp.int32, (512, 128), 1)
    spread = ((row // 8 == col % 64) & (row % 2 == col // 64)).astype(F32).astype(BF16)
    turned_row = (row // 2) % 2 == 1
    is_real = col % 64 < 32
    used = (row // 4) % 2 == col // 64
    zh = place[4]
    for win in range(8):
        base = (win * 4 + zh) * 2
        rows = jnp.concatenate([src_ref[base], src_ref[base + 1]], axis=0)
        plain = jnp.dot(spread, rows, preferred_element_type=F32)
        turned = jnp.where(
            is_real, -pltpu.roll(plain, 96, axis=1), pltpu.roll(plain, 32, axis=1)
        )
        left = jnp.where(used, jnp.where(turned_row, turned, plain), 0.0).astype(BF16)
        right = jnp.concatenate([rcv_ref[x * 8 + win] for x in range(4)], axis=0)
        part = lax.dot_general(left, right, (((1,), (1,)), ((), ())), preferred_element_type=F32)
        if win == 0:
            acc[...] = part
        else:
            acc[...] += part
    group = lax.broadcasted_iota(jnp.int32, (64, 128), 1) // 16
    for v in range(4):
        cols = slice(v * 128, v * 128 + 128)
        held = [acc[s * 64 : s * 64 + 64, cols] for s in range(8)]
        for bit in (4, 2, 1):
            low = (group & bit) == 0
            for s in range(8):
                if s & bit:
                    continue
                a, b = held[s], held[s + bit]
                held[s] = jnp.where(low, a, pltpu.roll(b, 16 * bit, axis=1))
                held[s + bit] = jnp.where(low, pltpu.roll(a, 128 - 16 * bit, axis=1), b)
        for g in range(8):
            first = (v * 8 + g) * 8
            out_ref[first : first + 8] = held[g].reshape(8, 8, 128).astype(BF16)


def cross_sums(place, src, rcv):
    return pl.pallas_call(
        cross_kernel,
        out_shape=jax.ShapeDtypeStruct((256, 8, 128), BF16),
        grid_spec=pltpu.PrefetchScalarGridSpec(
            num_scalar_prefetch=1,
            grid=(1,),
            in_specs=[
                pl.BlockSpec(src.shape, lambda i, p: (0, 0, 0)),
                pl.BlockSpec(rcv.shape, lambda i, p: (0, 0, 0)),
            ],
            out_specs=pl.BlockSpec((256, 8, 128), lambda i, p: (0, 0, 0)),
            scratch_shapes=[pltpu.VMEM((512, 512), F32)],
        ),
        compiler_params=pltpu.CompilerParams(vmem_limit_bytes=VMEM),
    )(place, src, rcv)


def lag_kernel(cross_ref, high_ref, low_ref, out_ref, wide, sorted_ref):
    @pl.when(pl.program_id(0) == 0)
    def _():
        wide[...] = cross_ref[...].astype(F32).reshape(2048, 128)
        for b in range(8):
            rows = wide[pl.ds(b, 256, stride=8), :].astype(BF16)
            sorted_ref[b // 2, :, b % 2 * 128 : b % 2 * 128 + 128] = rows

    total = None
    for b in range(4):
        for table in (high_ref, low_ref):
            part = lax.dot_general(
                sorted_ref[b],
                table[b * 256 : b * 256 + 256, :],
                (((0,), (0,)), ((), ())),
                preferred_element_type=F32,
            )
            total = part if total is None else total + part
    out_ref[...] = total


def to_lags(cross, high, low):
    return pl.pallas_call(
        lag_kernel,
        out_shape=jax.ShapeDtypeStruct((256, LAGS), F32),
        grid=(4,),
        in_specs=[
            pl.BlockSpec((256, 8, 128), lambda i: (0, 0, 0)),
            pl.BlockSpec((1024, 256), lambda i: (0, i)),
            pl.BlockSpec((1024, 256), lambda i: (0, i)),
        ],
        out_specs=pl.BlockSpec((256, 256), lambda i: (0, i)),
        scratch_shapes=[pltpu.VMEM((2048, 128), F32), pltpu.VMEM((4, 256, 256), BF16)],
        compiler_params=pltpu.CompilerParams(vmem_limit_bytes=VMEM),
    )(cross, high, low)


def inverse_table():
    x, zh, core, win = np.meshgrid(
        np.arange(4), np.arange(4), np.arange(2), np.arange(8), indexing="ij"
    )
    place = (x * 128 + (win * 4 + zh) * 2 + core).reshape(-1)
    lag = np.arange(LAGS)
    rows = []
    for j in range(2):
        freq = place + 64 * j
        phase = (freq[:, None] * lag[None, :] % LAGS) * (2.0 * math.pi / LAGS)
        weight = np.where(freq == 0, 1.0, 2.0)[:, None] / math.sqrt(WINDOWS * LAGS)
        rows += [weight * np.cos(phase), -weight * np.sin(phase)]
    table = np.concatenate(rows, axis=0).astype(np.float32)
    high = table.astype(BF16)
    low = (table - high.astype(np.float32)).astype(BF16)
    return jnp.asarray(high), jnp.asarray(low)


def exchange(x, core, pieces, receiver_spectra, bad_channels, place):
    far_low, far_high, up, down, own = pieces

    def hop(piece, start, step):
        pair = (start % 4 * 2 + core, (start + step) % 4 * 2 + core)
        return lax.ppermute(piece, ("x", "core"), [pair])

    far_low, far_high = hop(far_low, x, 1), hop(far_high, x, -1)
    up, down = hop(up, x, 1), hop(down, x, -1)
    blocks = receiver_blocks(receiver_spectra, place, bad_channels)
    rcv_at = lax.all_to_all(blocks, ("x", "y", "zl", "zh", "core"), 0, 0, tiled=True)
    far_low, far_high, _ = lax.optimization_barrier((far_low, far_high, blocks))
    far_low, far_high = hop(far_low, x + 1, 1), hop(far_high, x - 1, -1)
    pieces = (far_low, far_high, up, down, own)
    other = 1 - core
    shared = lax.ppermute(share(other, place, pieces), "core", [(core, other)])
    return turn_source(core, place, pieces, shared), rcv_at


def on_device(source_spectra, receiver_spectra, source_block, bad_channels):
    x, zh, core = (lax.axis_index(a) for a in ("x", "zh", "core"))
    holder = source_block[0]
    place = jnp.stack(
        [x, (x * 4 + zh) * 2 + core, core, (x - holder // 8) % 4, (holder // 2) % 4]
    ).astype(jnp.int32)
    src_blocks, rcv_at = lax.switch(
        holder // 8 * 2 + holder % 2,
        [functools.partial(exchange, i // 2, i % 2) for i in range(8)],
        tuple(source_pieces(source_spectra, place)),
        receiver_spectra,
        bad_channels,
        place,
    )
    src_at = lax.all_to_all(src_blocks, ("y", "zl", "zh", "core"), 0, 0, tiled=True)
    sums = cross_sums(place, src_at, rcv_at.reshape(32, 128, 128))
    mine = lax.all_to_all(sums, ("x", "zh", "core", "y", "zl"), 0, 0, tiled=True)
    high, low = inverse_table()
    return to_lags(mine, high, low).reshape(16, 16, LAGS)


def solution(mesh):
    fine = Mesh(mesh.devices.reshape(SIZES), AXES)
    win, rcv = AXES[:2], AXES[2:]
    return jax.shard_map(
        on_device,
        mesh=fine,
        in_specs=(P(win, rcv, None), P(win, rcv, None), P(), P()),
        out_specs=P(win, rcv, None),
        check_vma=False,
    )
```

profile of v0, /device:TPU:1, one launch (start us, length us, event | category | flops | bytes accessed | tf_op | source)
XLA Modules:
  0.0 154.8 jit_solution(3551286656450647766)
XLA Ops:
  0.7 0.1 stack.23.place
  0.8 0.0 copy-start
  0.8 0.0 copy-start.9
  0.8 10.8 %shard_map.64 = (bf16[16,128,256]{2,1,0:T(8,128)(2,1)}, bf16[16,128,256]{2,1,0:T(8,128)(2,1)}, bf16[32,128,256]{2,1,0:T(8,128)(2,1)}, bf16[32,128,256]{2,1,0:T(8,128)(2,1)}, bf16[32,128,256]{2,1,0:T(8,128)(2,1)S(1)}) custom-call(s32[5]{0:T(128)S(1)} %stack.23.place, bf16[32,128,1024]{2,1,0:T(8,128)(2,1)} %src_ref.1), custom_call_target="tpu_custom_call" | custom-call | flops 40000000 | bytes 16777216 | tf_op jit(solution)/shard_map/pallas_call | solution.py:70
  11.7 0.0 copy-done
  11.7 0.0 copy-done.9
  11.7 67.4 %conditional.1 = (bf16[64,64,128]{2,1,0:T(8,128)(2,1)S(1)}, bf16[32,128,128]{2,1,0:T(8,128)(2,1)}) conditional(s32[]{:T(128)} %clamp.3, (bf16[16,128,256]{2,1,0:T(8,128)(2,1)}, bf16[16,128,256]{2,1,0:T(8,128)(2,1)}, s32[5]{0:T(128)S(1)}, s32[64]{0:T(128)S(1)}, bf16[32,16,1024]{2,1,0:T(8,128)(2,1)S(1)}, ...), branch_computations={%region_0.1_spmd, %region_1.2_spmd, %region_2.3_spmd, %region_3.4_... | conditional | flops 20000000 | bytes 47186276 | solution.py:397
  11.9 1.6 %collective-permute-start.35 = (bf16[16,128,256]{2,1,0:T(8,128)(2,1)}, bf16[16,128,256]{2,1,0:T(8,128)(2,1)}, u32[]{:S(2)}, u32[]{:S(2)}) collective-permute-start(bf16[16,128,256]{2,1,0:T(8,128)(2,1)} %get-tuple-element.185), channel_id=1, source_target_pairs={{17,25},{19,27},{21,29},{23,31},{49,57},{51,59},{53,61},{55,63},{8... | collective-permute-start | bytes 3145736 | tf_op jit(solution)/shard_map/cond/branch_5_fun/ppermute | solution.py:377
  13.5 1.7 %collective-permute-start.36 = (bf16[16,128,256]{2,1,0:T(8,128)(2,1)}, bf16[16,128,256]{2,1,0:T(8,128)(2,1)}, u32[]{:S(2)}, u32[]{:S(2)}) collective-permute-start(bf16[16,128,256]{2,1,0:T(8,128)(2,1)} %get-tuple-element.186), channel_id=1, source_target_pairs={{17,9},{19,11},{21,13},{23,15},{49,41},{51,43},{53,45},{55,47},{81... | collective-permute-start | bytes 3145736 | tf_op jit(solution)/shard_map/cond/branch_5_fun/ppermute | solution.py:377
  15.2 2.0 %collective-permute-start.39 = (bf16[32,128,256]{2,1,0:T(8,128)(2,1)}, bf16[32,128,256]{2,1,0:T(8,128)(2,1)}, u32[]{:S(2)}, u32[]{:S(2)}) collective-permute-start(bf16[32,128,256]{2,1,0:T(8,128)(2,1)} %get-tuple-element.191), channel_id=1, source_target_pairs={{17,25},{19,27},{21,29},{23,31},{49,57},{51,59},{53,61},{55,63},{8... | collective-permute-start | bytes 6291464 | tf_op jit(solution)/shard_map/cond/branch_5_fun/ppermute | solution.py:377
  17.2 2.1 %collective-permute-start.40 = (bf16[32,128,256]{2,1,0:T(8,128)(2,1)}, bf16[32,128,256]{2,1,0:T(8,128)(2,1)}, u32[]{:S(2)}, u32[]{:S(2)}) collective-permute-start(bf16[32,128,256]{2,1,0:T(8,128)(2,1)} %get-tuple-element.192), channel_id=1, source_target_pairs={{17,9},{19,11},{21,13},{23,15},{49,41},{51,43},{53,45},{55,47},{81... | collective-permute-start | bytes 6291464 | tf_op jit(solution)/shard_map/cond/branch_5_fun/ppermute | solution.py:377
  19.2 4.5 %branch_5_fun.3 = bf16[256,16,128]{2,1,0:T(8,128)(2,1)} custom-call(s32[5]{0:T(128)S(1)} %get-tuple-element.184.place, s32[64]{0:T(128)S(1)} %get-tuple-element.187.bad, bf16[32,16,1024]{2,1,0:T(8,128)(2,1)S(1)} %get-tuple-element.188.rcv_ref), custom_call_target="tpu_custom_call" | custom-call | flops 20000000 | bytes 2097152 | tf_op jit(solution)/shard_map/cond/branch_5_fun/pallas_call | solution.py:137
  23.7 0.0 collective-permute-done.35
  23.7 0.0 collective-permute-done.36
  23.7 1.3 collective-permute-start.37
  25.0 1.3 collective-permute-start.38
  26.3 21.9 %all-to-all-start.5 = ((bf16[256,16,128]{2,1,0:T(8,128)(2,1)}), bf16[256,16,128]{2,1,0:T(8,128)(2,1)}, u32[]{:S(2)}, u32[]{:S(2)}) async-start(bf16[256,16,128]{2,1,0:T(8,128)(2,1)} %branch_5_fun.3), calls=%async_computation.5 | async-start | bytes 2097152 | tf_op jit(solution)/shard_map/cond/branch_5_fun/all_to_all | solution.py:382
  48.2 0.0 collective-permute-done.37.refs_0_
  48.2 0.0 copy-start.6
  48.2 0.0 collective-permute-done.38.refs_1_
  48.2 0.0 collective-permute-done.39.refs_2_
  48.2 0.0 collective-permute-done.40.refs_3_
  48.2 0.9 copy-done.6
  49.2 2.7 %branch_5_fun.4 = bf16[32,64,256]{2,1,0:T(8,128)(2,1)} custom-call(s32[5]{0:T(128)S(1)} %get-tuple-element.184.place, bf16[16,128,256]{2,1,0:T(8,128)(2,1)} %copy-done.6, bf16[16,128,256]{2,1,0:T(8,128)(2,1)} %collective-permute-done.38.refs_1_, bf16[32,128,256]{2,1,0:T(8,128)(2,1)} %collective-permute-done.39.refs_2_, ...), custom_call_target="tpu_custom_call" | custom-call | tf_op jit(solution)/shard_map/cond/branch_5_fun/pallas_call | solution.py:185
  51.9 5.1 %collective-permute-start.41 = (bf16[32,64,256]{2,1,0:T(8,128)(2,1)}, bf16[32,64,256]{2,1,0:T(8,128)(2,1)}, u32[]{:S(2)}, u32[]{:S(2)}) collective-permute-start(bf16[32,64,256]{2,1,0:T(8,128)(2,1)} %branch_5_fun.4), channel_id=1, source_target_pairs={{1,0},{3,2},{5,4},{7,6},{9,8},{11,10},{13,12},{15,14},{17,16},{19,... | collective-permute-start | bytes 3145736 | tf_op jit(solution)/shard_map/cond/branch_5_fun/ppermute | solution.py:387
  57.1 1.6 %collective-permute-done.41.refs_5_ = bf16[32,64,256]{2,1,0:T(8,128)(2,1)} collective-permute-done((bf16[32,64,256]{2,1,0:T(8,128)(2,1)}, bf16[32,64,256]{2,1,0:T(8,128)(2,1)}, u32[]{:S(2)}, u32[]{:S(2)}) %collective-permute-start.41) | collective-permute-done | bytes 1048608 | tf_op jit(solution)/shard_map/cond/branch_5_fun/ppermute | solution.py:387
  58.7 5.6 %branch_5_fun.5 = bf16[64,64,128]{2,1,0:T(8,128)(2,1)S(1)} custom-call(s32[5]{0:T(128)S(1)} %get-tuple-element.184.place, bf16[16,128,256]{2,1,0:T(8,128)(2,1)} %copy-done.6, bf16[16,128,256]{2,1,0:T(8,128)(2,1)} %collective-permute-done.38.refs_1_, bf16[32,128,256]{2,1,0:T(8,128)(2,1)} %collective-permute-done.39.refs_2_, ...), custom_call_target="tpu_custom_call" | custom-call | tf_op jit(solution)/shard_map/cond/branch_5_fun/pallas_call | solution.py:241
  64.3 14.8 %all-to-all-done.5 = bf16[256,16,128]{2,1,0:T(8,128)(2,1)} async-done(((bf16[256,16,128]{2,1,0:T(8,128)(2,1)}), bf16[256,16,128]{2,1,0:T(8,128)(2,1)}, u32[]{:S(2)}, u32[]{:S(2)}) %all-to-all-start.5) | async-done | bytes 1048608 | tf_op jit(solution)/shard_map/cond/branch_5_fun/all_to_all | solution.py:382
  79.1 33.6 %all_to_all.42.src_ref = bf16[64,64,128]{2,1,0:T(8,128)(2,1)} all-to-all(bf16[64,64,128]{2,1,0:T(8,128)(2,1)S(1)} %get-tuple-element.226), channel_id=1, replica_groups=mesh['y'=4,'zl'=2,'x'=4,'zh'=4,'core'=2] {'y','zl','zh','core'}, dimensions={0} | all-to-all | bytes 2097152 | tf_op jit(solution)/shard_map/all_to_all | solution.py:405
  112.7 6.2 %shard_map.65 = bf16[256,8,128]{2,1,0:T(8,128)(2,1)} custom-call(s32[5]{0:T(128)S(1)} %stack.23.place, bf16[64,64,128]{2,1,0:T(8,128)(2,1)} %all_to_all.42.src_ref, bf16[32,128,128]{2,1,0:T(8,128)(2,1)} %get-tuple-element.227.rcv_ref), custom_call_target="tpu_custom_call" | custom-call | tf_op jit(solution)/shard_map/pallas_call | solution.py:300
  118.8 30.7 %all_to_all.43.cross_ref = bf16[256,8,128]{2,1,0:T(8,128)(2,1)} all-to-all(bf16[256,8,128]{2,1,0:T(8,128)(2,1)} %shard_map.65), channel_id=1, replica_groups=mesh['y'=4,'zl'=2,'x'=4,'zh'=4,'core'=2] {'x','zh','core','y','zl'}, dimensions={0} | all-to-all | bytes 1048576 | tf_op jit(solution)/shard_map/all_to_all | solution.py:407
  149.5 5.3 %shard_map.66 = f32[256,1024]{1,0:T(8,128)} custom-call(bf16[256,8,128]{2,1,0:T(8,128)(2,1)} %all_to_all.43.cross_ref, bf16[1024,1024]{1,0:T(8,128)(2,1)} %constant.67.clone.high_ref, bf16[1024,1024]{1,0:T(8,128)(2,1)} %constant.68.clone.low_ref), custom_call_target="tpu_custom_call" | custom-call | tf_op jit(solution)/shard_map/pallas_call | solution.py:339
Async XLA Ops:
  0.8 10.8 %copy-start = (bf16[32,16,1024]{2,1,0:T(8,128)(2,1)S(1)}, bf16[32,16,1024]{2,1,0:T(8,128)(2,1)}, u32[]{:S(2)}) copy-start(bf16[32,16,1024]{2,1,0:T(8,128)(2,1)} %param.15) | copy-start | bytes 3145732
  0.8 10.8 %copy-start.9 = (s32[64]{0:T(128)S(1)}, s32[64]{0:T(128)}, u32[]{:S(2)}) copy-start(s32[64]{0:T(128)} %param.17) | copy-start | bytes 772
  11.9 11.8 %collective-permute-start.35 = (bf16[16,128,256]{2,1,0:T(8,128)(2,1)}, bf16[16,128,256]{2,1,0:T(8,128)(2,1)}, u32[]{:S(2)}, u32[]{:S(2)}) collective-permute-start(bf16[16,128,256]{2,1,0:T(8,128)(2,1)} %get-tuple-element.185), channel_id=1, source_target_pairs={{17,25},{19,27},{21,29},{23,31},{49,57},{51,59},{53,61},{55,63},{8... | collective-permute-start | bytes 3145736 | tf_op jit(solution)/shard_map/cond/branch_5_fun/ppermute | solution.py:377
  13.5 10.2 %collective-permute-start.36 = (bf16[16,128,256]{2,1,0:T(8,128)(2,1)}, bf16[16,128,256]{2,1,0:T(8,128)(2,1)}, u32[]{:S(2)}, u32[]{:S(2)}) collective-permute-start(bf16[16,128,256]{2,1,0:T(8,128)(2,1)} %get-tuple-element.186), channel_id=1, source_target_pairs={{17,9},{19,11},{21,13},{23,15},{49,41},{51,43},{53,45},{55,47},{81... | collective-permute-start | bytes 3145736 | tf_op jit(solution)/shard_map/cond/branch_5_fun/ppermute | solution.py:377
  15.2 33.0 %collective-permute-start.39 = (bf16[32,128,256]{2,1,0:T(8,128)(2,1)}, bf16[32,128,256]{2,1,0:T(8,128)(2,1)}, u32[]{:S(2)}, u32[]{:S(2)}) collective-permute-start(bf16[32,128,256]{2,1,0:T(8,128)(2,1)} %get-tuple-element.191), channel_id=1, source_target_pairs={{17,25},{19,27},{21,29},{23,31},{49,57},{51,59},{53,61},{55,63},{8... | collective-permute-start | bytes 6291464 | tf_op jit(solution)/shard_map/cond/branch_5_fun/ppermute | solution.py:377
  17.2 31.1 %collective-permute-start.40 = (bf16[32,128,256]{2,1,0:T(8,128)(2,1)}, bf16[32,128,256]{2,1,0:T(8,128)(2,1)}, u32[]{:S(2)}, u32[]{:S(2)}) collective-permute-start(bf16[32,128,256]{2,1,0:T(8,128)(2,1)} %get-tuple-element.192), channel_id=1, source_target_pairs={{17,9},{19,11},{21,13},{23,15},{49,41},{51,43},{53,45},{55,47},{81... | collective-permute-start | bytes 6291464 | tf_op jit(solution)/shard_map/cond/branch_5_fun/ppermute | solution.py:377
  23.7 24.5 %collective-permute-start.37 = (bf16[16,128,256]{2,1,0:T(8,128)(2,1)}, bf16[16,128,256]{2,1,0:T(8,128)(2,1)S(1)}, u32[]{:S(2)}, u32[]{:S(2)}) collective-permute-start(bf16[16,128,256]{2,1,0:T(8,128)(2,1)} %collective-permute-done.35), channel_id=1, source_target_pairs={{25,1},{27,3},{29,5},{31,7},{57,33},{59,35},{61,37},{63,39},{89,65... | collective-permute-start | bytes 3145736 | tf_op jit(solution)/shard_map/cond/branch_5_fun/ppermute | solution.py:377
  25.0 23.2 %collective-permute-start.38 = (bf16[16,128,256]{2,1,0:T(8,128)(2,1)}, bf16[16,128,256]{2,1,0:T(8,128)(2,1)}, u32[]{:S(2)}, u32[]{:S(2)}) collective-permute-start(bf16[16,128,256]{2,1,0:T(8,128)(2,1)} %collective-permute-done.36), channel_id=1, source_target_pairs={{9,1},{11,3},{13,5},{15,7},{41,33},{43,35},{45,37},{47,39},{73,65}... | collective-permute-start | bytes 3145736 | tf_op jit(solution)/shard_map/cond/branch_5_fun/ppermute | solution.py:377
  26.3 52.8 %all-to-all-start.5 = ((bf16[256,16,128]{2,1,0:T(8,128)(2,1)}), bf16[256,16,128]{2,1,0:T(8,128)(2,1)}, u32[]{:S(2)}, u32[]{:S(2)}) async-start(bf16[256,16,128]{2,1,0:T(8,128)(2,1)} %branch_5_fun.3), calls=%async_computation.5 | async-start | bytes 2097152 | tf_op jit(solution)/shard_map/cond/branch_5_fun/all_to_all | solution.py:382
  48.2 1.0 copy-start.6
  51.9 6.7 %collective-permute-start.41 = (bf16[32,64,256]{2,1,0:T(8,128)(2,1)}, bf16[32,64,256]{2,1,0:T(8,128)(2,1)}, u32[]{:S(2)}, u32[]{:S(2)}) collective-permute-start(bf16[32,64,256]{2,1,0:T(8,128)(2,1)} %branch_5_fun.4), channel_id=1, source_target_pairs={{1,0},{3,2},{5,4},{7,6},{9,8},{11,10},{13,12},{15,14},{17,16},{19,... | collective-permute-start | bytes 3145736 | tf_op jit(solution)/shard_map/cond/branch_5_fun/ppermute | solution.py:387
where the time goes:
time: 156 us; the launch traced here: 155 us
  blocking collectives  64.3 us (41%)
  starting transfers between devices  37 us (24%)
  Pallas kernels  35.1 us (22%)
  waiting for transfers between devices  16.4 us (11%)
    all_to_all x1, blocking collectives, on_device(): lax.all_to_all(src_blocks, ('y', 'zl', 'zh', 'core'), 0, 0, tiled=True)  33.6 us
    all_to_all x1, blocking collectives, on_device(): lax.all_to_all(sums, ('x', 'zh', 'core', 'y', 'zl'), 0, 0, tiled=True)  30.7 us
    all_to_all x1, starting transfers between devices, exchange(): lax.all_to_all(blocks, ('x', 'y', 'zl', 'zh', 'core'), 0, 0, tiled=True)  21.9 us
    all_to_all x1, waiting for transfers between devices, exchange(): lax.all_to_all(blocks, ('x', 'y', 'zl', 'zh', 'core'), 0, 0, tiled=True)  14.8 us
    pallas_call x1, Pallas kernels, source_pieces(): pl.pallas_call(source_kernel, out_shape=[part] * 2 + [piece] * 3, grid_sp...  10.8 us
    ppermute x6, starting transfers between devices, hop(): return lax.ppermute(piece, ('x', 'core'), [pair])  9.94 us
    pallas_call x1, Pallas kernels, cross_sums(): pl.pallas_call(cross_kernel, out_shape=jax.ShapeDtypeStruct((256, 8, 128)...  6.18 us
    pallas_call x1, Pallas kernels, turn_source(): pl.pallas_call(functools.partial(turn_kernel, holder_core), out_shape=jax...  5.58 us
  transfers between devices with their start and end apart: 8, of which 2 were waited for; matrix products, arithmetic and copies ran while one was open for 0% of the time, Pallas kernels for 8%

commit v1 on v0

--- a/solution.py
+++ b/solution.py
@@ -115,6 +115,7 @@
 
     @pl.loop(0, 4)
     def _(q):
+        ahead = lax.rem(q + 4 - place[0], 4)
         for c in range(0, chans, 2):
             pair = turn_pair(
                 *(
@@ -124,24 +125,24 @@
                 )
             )
             for i in range(2):
-                turned[pl.ds(q * 64 * chans + c + i, 64, stride=chans), :] = pair[i]
+                turned[pl.ds(ahead * chans + c + i, 64, stride=4 * chans), :] = pair[i]
 
     @pl.loop(0, 8)
     def _(j):
         rows = turned[pl.ds(pl.multiple_of(j * 32 * chans, 32 * chans), 32 * chans), :]
-        out_ref[pl.ds(j * 32, 32)] = rows.reshape(32, chans, 128).astype(BF16)
+        out_ref[pl.ds(j * 8, 8)] = rows.reshape(8, 4 * chans, 128).astype(BF16)
 
 
 def receiver_blocks(rcv, place, bad):
     windows, chans, _ = rcv.shape
     return pl.pallas_call(
         receiver_kernel,
-        out_shape=jax.ShapeDtypeStruct((256, chans, 128), BF16),
+        out_shape=jax.ShapeDtypeStruct((64, 4 * chans, 128), BF16),
         grid_spec=pltpu.PrefetchScalarGridSpec(
             num_scalar_prefetch=2,
             grid=(1,),
             in_specs=[pl.BlockSpec(rcv.shape, lambda i, p, b: (0, 0, 0))],
-            out_specs=pl.BlockSpec((256, chans, 128), lambda i, p, b: (0, 0, 0)),
+            out_specs=pl.BlockSpec((64, 4 * chans, 128), lambda i, p, b: (0, 0, 0)),
             scratch_shapes=[
                 pltpu.VMEM((8, windows * chans, 128), F32),
                 pltpu.VMEM((256 * chans, 128), F32),
@@ -257,32 +258,33 @@
     )(place, *pieces, shared)
 
 
-def cross_kernel(place, src_ref, rcv_ref, out_ref, acc):
-    row = lax.broadcasted_iota(jnp.int32, (512, 128), 0)
-    col = lax.broadcasted_iota(jnp.int32, (512, 128), 1)
-    spread = ((row // 8 == col % 64) & (row % 2 == col // 64)).astype(F32).astype(BF16)
-    turned_row = (row // 2) % 2 == 1
-    is_real = col % 64 < 32
-    used = (row // 4) % 2 == col // 64
+def cross_kernel(place, src_ref, *refs):
+    rcv_refs, out_ref, left = refs[:4], refs[4], refs[5]
+    row = lax.broadcasted_iota(jnp.int32, (512, 256), 0)
+    col = lax.broadcasted_iota(jnp.int32, (512, 256), 1)
+    wanted = ((row // 2) % 2) * 128 + (row % 2) * 64 + row // 8
+    spread = (wanted == col).astype(F32).astype(BF16)
+    lane = lax.broadcasted_iota(jnp.int32, (512, 128), 1)
+    used = (lax.broadcasted_iota(jnp.int32, (512, 128), 0) // 4) % 2 == lane // 64
+    is_real = lane[:128] % 64 < 32
     zh = place[4]
     for win in range(8):
         base = (win * 4 + zh) * 2
-        rows = jnp.concatenate([src_ref[base], src_ref[base + 1]], axis=0)
-        plain = jnp.dot(spread, rows, preferred_element_type=F32)
-        turned = jnp.where(
-            is_real, -pltpu.roll(plain, 96, axis=1), pltpu.roll(plain, 32, axis=1)
+        plain = jnp.concatenate([src_ref[base], src_ref[base + 1]], axis=0)
+        wide = plain.astype(F32)
+        turned = jnp.where(is_real, -pltpu.roll(wide, 96, axis=1), pltpu.roll(wide, 32, axis=1))
+        both = jnp.concatenate([plain, turned.astype(BF16)], axis=0)
+        rows = jnp.dot(spread, both, preferred_element_type=F32)
+        left[:, win * 128 : win * 128 + 128] = jnp.where(used, rows, 0.0).astype(BF16)
+    group = lax.broadcasted_iota(jnp.int32, (64, 128), 1) // 16
+    for ahead in range(4):
+        right = jnp.concatenate(
+            [rcv_refs[ahead][w * 8 : w * 8 + 8].reshape(128, 128) for w in range(8)], axis=1
         )
-        left = jnp.where(used, jnp.where(turned_row, turned, plain), 0.0).astype(BF16)
-        right = jnp.concatenate([rcv_ref[x * 8 + win] for x in range(4)], axis=0)
-        part = lax.dot_general(left, right, (((1,), (1,)), ((), ())), preferred_element_type=F32)
-        if win == 0:
-            acc[...] = part
-        else:
-            acc[...] += part
-    group = lax.broadcasted_iota(jnp.int32, (64, 128), 1) // 16
-    for v in range(4):
-        cols = slice(v * 128, v * 128 + 128)
-        held = [acc[s * 64 : s * 64 + 64, cols] for s in range(8)]
+        sums = lax.dot_general(
+            left[...], right, (((1,), (1,)), ((), ())), preferred_element_type=F32
+        )
+        held = [sums[s * 64 : s * 64 + 64] for s in range(8)]
         for bit in (4, 2, 1):
             low = (group & bit) == 0
             for s in range(8):
@@ -291,48 +293,39 @@
                 a, b = held[s], held[s + bit]
                 held[s] = jnp.where(low, a, pltpu.roll(b, 16 * bit, axis=1))
                 held[s + bit] = jnp.where(low, pltpu.roll(a, 128 - 16 * bit, axis=1), b)
+        first = lax.rem(place[0] + 4 - ahead, 4) * 64
         for g in range(8):
-            first = (v * 8 + g) * 8
-            out_ref[first : first + 8] = held[g].reshape(8, 8, 128).astype(BF16)
-
-
-def cross_sums(place, src, rcv):
+            out_ref[pl.ds(first + g * 8, 8)] = held[g].reshape(8, 8, 128).astype(BF16)
+
+
+def cross_sums(place, src, rcvs):
     return pl.pallas_call(
         cross_kernel,
         out_shape=jax.ShapeDtypeStruct((256, 8, 128), BF16),
         grid_spec=pltpu.PrefetchScalarGridSpec(
             num_scalar_prefetch=1,
             grid=(1,),
-            in_specs=[
-                pl.BlockSpec(src.shape, lambda i, p: (0, 0, 0)),
-                pl.BlockSpec(rcv.shape, lambda i, p: (0, 0, 0)),
-            ],
+            in_specs=[pl.BlockSpec(a.shape, lambda i, p: (0, 0, 0)) for a in (src, *rcvs)],
             out_specs=pl.BlockSpec((256, 8, 128), lambda i, p: (0, 0, 0)),
-            scratch_shapes=[pltpu.VMEM((512, 512), F32)],
-        ),
-        compiler_params=pltpu.CompilerParams(vmem_limit_bytes=VMEM),
-    )(place, src, rcv)
-
-
-def lag_kernel(cross_ref, high_ref, low_ref, out_ref, wide, sorted_ref):
+            scratch_shapes=[pltpu.VMEM((512, 1024), BF16)],
+        ),
+        compiler_params=pltpu.CompilerParams(vmem_limit_bytes=VMEM),
+    )(place, src, *rcvs)
+
+
+def lag_kernel(cross_ref, high_ref, low_ref, out_ref, wide, sums):
     @pl.when(pl.program_id(0) == 0)
     def _():
         wide[...] = cross_ref[...].astype(F32).reshape(2048, 128)
         for b in range(8):
-            rows = wide[pl.ds(b, 256, stride=8), :].astype(BF16)
-            sorted_ref[b // 2, :, b % 2 * 128 : b % 2 * 128 + 128] = rows
-
-    total = None
-    for b in range(4):
-        for table in (high_ref, low_ref):
-            part = lax.dot_general(
-                sorted_ref[b],
-                table[b * 256 : b * 256 + 256, :],
-                (((0,), (0,)), ((), ())),
-                preferred_element_type=F32,
+            rows, cols = b % 2 * 128, b // 2 * 256
+            sums[rows : rows + 128, cols : cols + 256] = (
+                wide[pl.ds(b, 256, stride=8), :].T.astype(BF16)
             )
-            total = part if total is None else total + part
-    out_ref[...] = total
+
+    out_ref[...] = jnp.dot(sums[...], high_ref[...], preferred_element_type=F32) + jnp.dot(
+        sums[...], low_ref[...], preferred_element_type=F32
+    )
 
 
 def to_lags(cross, high, low):
@@ -346,7 +339,7 @@
             pl.BlockSpec((1024, 256), lambda i: (0, i)),
         ],
         out_specs=pl.BlockSpec((256, 256), lambda i: (0, i)),
-        scratch_shapes=[pltpu.VMEM((2048, 128), F32), pltpu.VMEM((4, 256, 256), BF16)],
+        scratch_shapes=[pltpu.VMEM((2048, 128), F32), pltpu.VMEM((256, 1024), BF16)],
         compiler_params=pltpu.CompilerParams(vmem_limit_bytes=VMEM),
     )(cross, high, low)
 
@@ -379,7 +372,7 @@
     far_low, far_high = hop(far_low, x, 1), hop(far_high, x, -1)
     up, down = hop(up, x, 1), hop(down, x, -1)
     blocks = receiver_blocks(receiver_spectra, place, bad_channels)
-    rcv_at = lax.all_to_all(blocks, ("x", "y", "zl", "zh", "core"), 0, 0, tiled=True)
+    rcv_at = lax.all_to_all(blocks, ("y", "zl", "zh", "core"), 0, 0, tiled=True)
     far_low, far_high, _ = lax.optimization_barrier((far_low, far_high, blocks))
     far_low, far_high = hop(far_low, x + 1, 1), hop(far_high, x - 1, -1)
     pieces = (far_low, far_high, up, down, own)
@@ -402,8 +395,12 @@
         bad_channels,
         place,
     )
+    chans = rcv_at.shape[1] // 4
+    rcvs = [rcv_at[:, i * chans : i * chans + chans] for i in range(4)]
+    for i in (2, 1, 3):
+        rcvs[i] = lax.ppermute(rcvs[i], "x", [(j, (j + i) % 4) for j in range(4)])
     src_at = lax.all_to_all(src_blocks, ("y", "zl", "zh", "core"), 0, 0, tiled=True)
-    sums = cross_sums(place, src_at, rcv_at.reshape(32, 128, 128))
+    sums = cross_sums(place, src_at, rcvs)
     mine = lax.all_to_all(sums, ("x", "zh", "core", "y", "zl"), 0, 0, tiled=True)
     high, low = inverse_table()
     return to_lags(mine, high, low).reshape(16, 16, LAGS)

time: 156 us -> 165 us (1.058)
  blocking collectives: 64.3 us -> 33 us
  starting transfers between devices: 37 us -> 62 us
  waiting for transfers between devices: 16.4 us -> 28.9 us
  local copies, waits for them, and re-layouts: 1.03 us -> 5.13 us
    all_to_all x1 -> x0, blocking collectives: 33.6 us -> none  [on_device(): lax.all_to_all(src_blocks, ('y', 'zl', 'zh', 'core'), 0, 0, tiled=True)]
    ppermute x0 -> x3, starting transfers between devices: none -> 29.7 us  [on_device(): rcvs[i] = lax.ppermute(rcvs[i], 'x', [(j, (j + i) % 4) for j in range(4)])]
    ppermute x0 -> x3, waiting for transfers between devices: none -> 13.5 us  [on_device(): rcvs[i] = lax.ppermute(rcvs[i], 'x', [(j, (j + i) % 4) for j in range(4)])]
    all_to_all x1 -> x2, waiting for transfers between devices: 14.8 us -> 4.08 us  [the longest x1 4.07 us: exchange(): rcv_at = lax.all_to_all(blocks, ('y', 'zl', 'zh', 'core'), 0, 0, tiled=True)]
    ppermute x1, waiting for transfers between devices: 1.6 us -> 11.4 us  [exchange(): shared = lax.ppermute(share(other, place, pieces), 'core', [(core, other)])]
    ppermute x1, starting transfers between devices: 5.15 us -> 1.29 us  [exchange(): shared = lax.ppermute(share(other, place, pieces), 'core', [(core, other)])]
    all_to_all x1, blocking collectives: 30.7 us -> 33 us  [on_device(): lax.all_to_all(sums, ('x', 'zh', 'core', 'y', 'zl'), 0, 0, tiled=True)]
    slice x0 -> x1, local copies, waits for them, and re-layouts: none -> 2.1 us  [on_device(): rcvs = [rcv_at[:, i * chans:i * chans + chans] for i in range(4)]]
  transfers between devices with their start and end apart: 8 -> 12, of which waited for: 2 -> 4; matrix products, arithmetic and copies ran while one was open for 0% -> 1% of each run, Pallas kernels for 8% -> 9%
where the time goes in v1:
time: 165 us
  starting transfers between devices  62 us (38%)
  Pallas kernels  35.1 us (21%)
  blocking collectives  33 us (20%)
  waiting for transfers between devices  28.9 us (18%)
  local copies, waits for them, and re-layouts  5.13 us (3%)
    all_to_all x1, blocking collectives, on_device(): lax.all_to_all(sums, ('x', 'zh', 'core', 'y', 'zl'), 0, 0, tiled=True)  33 us
    ppermute x3, starting transfers between devices, on_device(): rcvs[i] = lax.ppermute(rcvs[i], 'x', [(j, (j + i) % 4) for j in range(4)])  29.7 us
    all_to_all x1, starting transfers between devices, exchange(): rcv_at = lax.all_to_all(blocks, ('y', 'zl', 'zh', 'core'), 0, 0, tiled=True)  13.6 us
    ppermute x3, waiting for transfers between devices, on_device(): rcvs[i] = lax.ppermute(rcvs[i], 'x', [(j, (j + i) % 4) for j in range(4)])  13.5 us
    ppermute x1, waiting for transfers between devices, exchange(): shared = lax.ppermute(share(other, place, pieces), 'core', [(core, other)])  11.4 us
    pallas_call x1, Pallas kernels, source_pieces(): pl.pallas_call(source_kernel, out_shape=[part] * 2 + [piece] * 3, grid_sp...  10.8 us
    ppermute x6, starting transfers between devices, hop(): return lax.ppermute(piece, ('x', 'core'), [pair])  9.68 us
    all_to_all x1, starting transfers between devices, on_device(): lax.all_to_all(src_blocks, ('y', 'zl', 'zh', 'core'), 0, 0, tiled=True)  7.76 us
  transfers between devices with their start and end apart: 12, of which 4 were waited for; matrix products, arithmetic and copies ran while one was open for 1% of the time, Pallas kernels for 9%

profile of v1, /device:TPU:1, one launch (start us, length us, event | category | flops | bytes accessed | tf_op | source)
XLA Modules:
  0.0 165.1 jit_solution(16009456217892409553)
XLA Ops:
  0.7 0.1 stack.23.place
  0.8 0.0 copy-start
  0.8 10.8 %shard_map.64 = (bf16[16,128,256]{2,1,0:T(8,128)(2,1)}, bf16[16,128,256]{2,1,0:T(8,128)(2,1)}, bf16[32,128,256]{2,1,0:T(8,128)(2,1)}, bf16[32,128,256]{2,1,0:T(8,128)(2,1)}, bf16[32,128,256]{2,1,0:T(8,128)(2,1)S(1)}) custom-call(s32[5]{0:T(128)S(1)} %stack.23.place, bf16[32,128,1024]{2,1,0:T(8,128)(2,1)} %src_ref.1), custom_call_target="tpu_custom_call" | custom-call | flops 40000000 | bytes 16777216 | tf_op jit(solution)/shard_map/pallas_call | solution.py:70
  11.7 0.0 copy-done
  11.7 0.0 copy-done.21
  11.7 56.2 %conditional.1 = (bf16[64,64,128]{2,1,0:T(8,128)(2,1)}, bf16[64,64,128]{2,1,0:T(8,128)(2,1)}) conditional(s32[]{:T(128)} %clamp.3, (bf16[16,128,256]{2,1,0:T(8,128)(2,1)}, bf16[16,128,256]{2,1,0:T(8,128)(2,1)}, s32[5]{0:T(128)S(1)}, s32[64]{0:T(128)S(1)}, bf16[32,16,1024]{2,1,0:T(8,128)(2,1)S(1)}, ...), branch_computations={%region_0.1_spmd, %region_1.2_spmd, %region_2.3_spmd, %region_3.4_... | conditional | flops 20000000 | bytes 51380608 | solution.py:390
  11.9 1.6 collective-permute-start.28
  13.5 1.7 %collective-permute-start.29 = (bf16[16,128,256]{2,1,0:T(8,128)(2,1)}, bf16[16,128,256]{2,1,0:T(8,128)(2,1)}, u32[]{:S(2)}, u32[]{:S(2)}) collective-permute-start(bf16[16,128,256]{2,1,0:T(8,128)(2,1)} %get-tuple-element.175), channel_id=1, source_target_pairs={{16,8},{18,10},{20,12},{22,14},{48,40},{50,42},{52,44},{54,46},{80... | collective-permute-start | bytes 3145736 | tf_op jit(solution)/shard_map/cond/branch_4_fun/ppermute | solution.py:370
  15.2 2.0 %collective-permute-start.32 = (bf16[32,128,256]{2,1,0:T(8,128)(2,1)}, bf16[32,128,256]{2,1,0:T(8,128)(2,1)}, u32[]{:S(2)}, u32[]{:S(2)}) collective-permute-start(bf16[32,128,256]{2,1,0:T(8,128)(2,1)} %get-tuple-element.180), channel_id=1, source_target_pairs={{16,24},{18,26},{20,28},{22,30},{48,56},{50,58},{52,60},{54,62},{8... | collective-permute-start | bytes 6291464 | tf_op jit(solution)/shard_map/cond/branch_4_fun/ppermute | solution.py:370
  17.1 2.0 %collective-permute-start.33 = (bf16[32,128,256]{2,1,0:T(8,128)(2,1)}, bf16[32,128,256]{2,1,0:T(8,128)(2,1)}, u32[]{:S(2)}, u32[]{:S(2)}) collective-permute-start(bf16[32,128,256]{2,1,0:T(8,128)(2,1)} %get-tuple-element.181), channel_id=1, source_target_pairs={{16,8},{18,10},{20,12},{22,14},{48,40},{50,42},{52,44},{54,46},{80... | collective-permute-start | bytes 6291464 | tf_op jit(solution)/shard_map/cond/branch_4_fun/ppermute | solution.py:370
  19.2 4.6 %branch_4_fun.3 = bf16[64,64,128]{2,1,0:T(8,128)(2,1)} custom-call(s32[5]{0:T(128)S(1)} %get-tuple-element.173.place, s32[64]{0:T(128)S(1)} %get-tuple-element.176.bad, bf16[32,16,1024]{2,1,0:T(8,128)(2,1)S(1)} %get-tuple-element.177.rcv_ref), custom_call_target="tpu_custom_call" | custom-call | flops 20000000 | bytes 2097152 | tf_op jit(solution)/shard_map/cond/branch_4_fun/pallas_call | solution.py:138
  23.8 0.0 collective-permute-done.28
  23.8 0.0 collective-permute-done.29
  23.8 0.7 collective-permute-start.30
  24.6 1.6 collective-permute-start.31
  26.2 13.6 %all-to-all-start.4 = ((bf16[64,64,128]{2,1,0:T(8,128)(2,1)}), bf16[64,64,128]{2,1,0:T(8,128)(2,1)}, u32[]{:S(2)}, u32[]{:S(2)}) async-start(bf16[64,64,128]{2,1,0:T(8,128)(2,1)} %branch_4_fun.3), calls=%async_computation.4 | async-start | bytes 2097152 | tf_op jit(solution)/shard_map/cond/branch_4_fun/all_to_all | solution.py:375
  39.8 0.0 collective-permute-done.30.refs_0_
  39.8 0.0 copy-start.6
  39.8 0.0 collective-permute-done.31.refs_1_
  39.8 0.0 collective-permute-done.32.refs_2_
  39.8 0.0 collective-permute-done.33.refs_3_
  39.8 0.9 copy-done.6
  40.7 2.8 %branch_4_fun.4 = bf16[32,64,256]{2,1,0:T(8,128)(2,1)} custom-call(s32[5]{0:T(128)S(1)} %get-tuple-element.173.place, bf16[16,128,256]{2,1,0:T(8,128)(2,1)} %copy-done.6, bf16[16,128,256]{2,1,0:T(8,128)(2,1)} %collective-permute-done.31.refs_1_, bf16[32,128,256]{2,1,0:T(8,128)(2,1)} %collective-permute-done.32.refs_2_, ...), custom_call_target="tpu_custom_call" | custom-call | tf_op jit(solution)/shard_map/cond/branch_4_fun/pallas_call | solution.py:186
  43.5 1.3 collective-permute-start.34
  44.8 11.4 %collective-permute-done.34.refs_5_ = bf16[32,64,256]{2,1,0:T(8,128)(2,1)S(1)} collective-permute-done((bf16[32,64,256]{2,1,0:T(8,128)(2,1)}, bf16[32,64,256]{2,1,0:T(8,128)(2,1)S(1)}, u32[]{:S(2)}, u32[]{:S(2)}) %collective-permute-start.34) | collective-permute-done | bytes 1048608 | tf_op jit(solution)/shard_map/cond/branch_4_fun/ppermute | solution.py:380
  56.2 0.0 copy-start.14
  56.2 1.0 copy-done.14
  57.2 6.6 %branch_4_fun.5 = bf16[64,64,128]{2,1,0:T(8,128)(2,1)} custom-call(s32[5]{0:T(128)S(1)} %get-tuple-element.173.place, bf16[16,128,256]{2,1,0:T(8,128)(2,1)} %copy-done.6, bf16[16,128,256]{2,1,0:T(8,128)(2,1)} %collective-permute-done.31.refs_1_, bf16[32,128,256]{2,1,0:T(8,128)(2,1)} %collective-permute-done.32.refs_2_, ...), custom_call_target="tpu_custom_call" | custom-call | tf_op jit(solution)/shard_map/cond/branch_4_fun/pallas_call | solution.py:242
  63.8 4.1 %all-to-all-done.4 = bf16[64,64,128]{2,1,0:T(8,128)(2,1)} async-done(((bf16[64,64,128]{2,1,0:T(8,128)(2,1)}), bf16[64,64,128]{2,1,0:T(8,128)(2,1)}, u32[]{:S(2)}, u32[]{:S(2)}) %all-to-all-start.4) | async-done | bytes 1048608 | tf_op jit(solution)/shard_map/cond/branch_4_fun/all_to_all | solution.py:375
  67.9 7.8 %all-to-all-start.8 = ((bf16[64,64,128]{2,1,0:T(8,128)(2,1)}), bf16[64,64,128]{2,1,0:T(8,128)(2,1)S(1)}, u32[]{:S(2)}, u32[]{:S(2)}) async-start(bf16[64,64,128]{2,1,0:T(8,128)(2,1)} %get-tuple-element.225), calls=%async_computation.8 | async-start | bytes 2097152 | tf_op jit(solution)/shard_map/all_to_all | solution.py:402
  75.7 2.1 %fusion = (bf16[64,16,128]{2,1,0:T(8,128)(2,1)S(1)}, bf16[64,16,128]{2,1,0:T(8,128)(2,1)S(1)}, bf16[64,16,128]{2,1,0:T(8,128)(2,1)S(1)}, bf16[64,16,128]{2,1,0:T(8,128)(2,1)}) fusion(bf16[64,64,128]{2,1,0:T(8,128)(2,1)} %get-tuple-element.226), kind=kLoop, calls=%fused_computation | loop fusion | bytes 2097152 | tf_op jit(solution)/shard_map/slice | solution.py:399
  77.8 16.4 %collective-permute-start.58 = (bf16[64,16,128]{2,1,0:T(8,128)(2,1)S(1)}, bf16[64,16,128]{2,1,0:T(8,128)(2,1)S(1)}, u32[]{:S(2)}, u32[]{:S(2)}) collective-permute-start(bf16[64,16,128]{2,1,0:T(8,128)(2,1)S(1)} %get-tuple-element.227), channel_id=1, source_target_pairs={{0,24},{8,0},{16,8},{24,16},{1,25},{9,1},{17,9},{25,17},{2,26},{10... | collective-permute-start | bytes 786440 | tf_op jit(solution)/shard_map/ppermute | solution.py:401
  94.2 11.8 %collective-permute-start.57 = (bf16[64,16,128]{2,1,0:T(8,128)(2,1)S(1)}, bf16[64,16,128]{2,1,0:T(8,128)(2,1)S(1)}, u32[]{:S(2)}, u32[]{:S(2)}) collective-permute-start(bf16[64,16,128]{2,1,0:T(8,128)(2,1)S(1)} %get-tuple-element.228), channel_id=1, source_target_pairs={{0,16},{8,24},{16,0},{24,8},{1,17},{9,25},{17,1},{25,9},{2,18},{10... | collective-permute-start | bytes 786440 | tf_op jit(solution)/shard_map/ppermute | solution.py:401
  106.1 1.4 collective-permute-start.56
  107.4 0.0 collective-permute-done.58.refs_3_
  107.4 0.0 copy-start.18
  107.4 7.9 %collective-permute-done.57.refs_2_ = bf16[64,16,128]{2,1,0:T(8,128)(2,1)S(1)} collective-permute-done((bf16[64,16,128]{2,1,0:T(8,128)(2,1)S(1)}, bf16[64,16,128]{2,1,0:T(8,128)(2,1)S(1)}, u32[]{:S(2)}, u32[]{:S(2)}) %collective-permute-start.57) | collective-permute-done | bytes 262176 | tf_op jit(solution)/shard_map/ppermute | solution.py:401
  115.4 0.0 copy-start.19
  115.4 5.5 %collective-permute-done.56.refs_1_ = bf16[64,16,128]{2,1,0:T(8,128)(2,1)S(1)} collective-permute-done((bf16[64,16,128]{2,1,0:T(8,128)(2,1)S(1)}, bf16[64,16,128]{2,1,0:T(8,128)(2,1)S(1)}, u32[]{:S(2)}, u32[]{:S(2)}) %collective-permute-start.56) | collective-permute-done | bytes 262176 | tf_op jit(solution)/shard_map/ppermute | solution.py:401
  120.9 0.0 copy-start.20
  120.9 0.0 all-to-all-done.8.src_ref
  120.9 0.0 copy-done.18
  120.9 0.0 copy-done.19
  120.9 0.7 copy-done.20
  121.6 0.4 copy-done.1
  122.0 5.0 %shard_map.65 = bf16[256,8,128]{2,1,0:T(8,128)(2,1)} custom-call(s32[5]{0:T(128)S(1)} %stack.23.place, bf16[64,64,128]{2,1,0:T(8,128)(2,1)} %copy-done.1, bf16[64,16,128]{2,1,0:T(8,128)(2,1)} %get-tuple-element.230.refs_0_, bf16[64,16,128]{2,1,0:T(8,128)(2,1)} %copy-done.20, bf16[64,16,128]{2,1,0:T(8,128)(2,1)} %copy-done.19, bf16[64,16,128]{2,1,0:T(8,128)(2,1)} %copy-done.18), custom_call_target="tpu_custom_call" | custom-call | tf_op jit(solution)/shard_map/pallas_call | solution.py:302
  126.9 33.0 %all_to_all.42.cross_ref = bf16[256,8,128]{2,1,0:T(8,128)(2,1)} all-to-all(bf16[256,8,128]{2,1,0:T(8,128)(2,1)} %shard_map.65), channel_id=1, replica_groups=mesh['y'=4,'zl'=2,'x'=4,'zh'=4,'core'=2] {'x','zh','core','y','zl'}, dimensions={0} | all-to-all | bytes 1048576 | tf_op jit(solution)/shard_map/all_to_all | solution.py:404
  159.9 5.2 %shard_map.66 = f32[256,1024]{1,0:T(8,128)} custom-call(bf16[256,8,128]{2,1,0:T(8,128)(2,1)} %all_to_all.42.cross_ref, bf16[1024,1024]{1,0:T(8,128)(2,1)} %constant.67.clone.high_ref, bf16[1024,1024]{1,0:T(8,128)(2,1)} %constant.68.clone.low_ref), custom_call_target="tpu_custom_call" | custom-call | tf_op jit(solution)/shard_map/pallas_call | solution.py:332
  (2 shorter events, 0.0 us)
Async XLA Ops:
  0.8 10.8 %copy-start = (bf16[32,16,1024]{2,1,0:T(8,128)(2,1)S(1)}, bf16[32,16,1024]{2,1,0:T(8,128)(2,1)}, u32[]{:S(2)}) copy-start(bf16[32,16,1024]{2,1,0:T(8,128)(2,1)} %param.15) | copy-start | bytes 3145732
  0.8 10.8 %copy-start.21 = (s32[64]{0:T(128)S(1)}, s32[64]{0:T(128)}, u32[]{:S(2)}) copy-start(s32[64]{0:T(128)} %param.17) | copy-start | bytes 772
  11.9 11.9 %collective-permute-start.28 = (bf16[16,128,256]{2,1,0:T(8,128)(2,1)}, bf16[16,128,256]{2,1,0:T(8,128)(2,1)}, u32[]{:S(2)}, u32[]{:S(2)}) collective-permute-start(bf16[16,128,256]{2,1,0:T(8,128)(2,1)} %get-tuple-element.174), channel_id=1, source_target_pairs={{16,24},{18,26},{20,28},{22,30},{48,56},{50,58},{52,60},{54,62},{8... | collective-permute-start | bytes 3145736 | tf_op jit(solution)/shard_map/cond/branch_4_fun/ppermute | solution.py:370
  13.5 10.3 %collective-permute-start.29 = (bf16[16,128,256]{2,1,0:T(8,128)(2,1)}, bf16[16,128,256]{2,1,0:T(8,128)(2,1)}, u32[]{:S(2)}, u32[]{:S(2)}) collective-permute-start(bf16[16,128,256]{2,1,0:T(8,128)(2,1)} %get-tuple-element.175), channel_id=1, source_target_pairs={{16,8},{18,10},{20,12},{22,14},{48,40},{50,42},{52,44},{54,46},{80... | collective-permute-start | bytes 3145736 | tf_op jit(solution)/shard_map/cond/branch_4_fun/ppermute | solution.py:370
  15.2 24.6 %collective-permute-start.32 = (bf16[32,128,256]{2,1,0:T(8,128)(2,1)}, bf16[32,128,256]{2,1,0:T(8,128)(2,1)}, u32[]{:S(2)}, u32[]{:S(2)}) collective-permute-start(bf16[32,128,256]{2,1,0:T(8,128)(2,1)} %get-tuple-element.180), channel_id=1, source_target_pairs={{16,24},{18,26},{20,28},{22,30},{48,56},{50,58},{52,60},{54,62},{8... | collective-permute-start | bytes 6291464 | tf_op jit(solution)/shard_map/cond/branch_4_fun/ppermute | solution.py:370
  17.1 22.7 %collective-permute-start.33 = (bf16[32,128,256]{2,1,0:T(8,128)(2,1)}, bf16[32,128,256]{2,1,0:T(8,128)(2,1)}, u32[]{:S(2)}, u32[]{:S(2)}) collective-permute-start(bf16[32,128,256]{2,1,0:T(8,128)(2,1)} %get-tuple-element.181), channel_id=1, source_target_pairs={{16,8},{18,10},{20,12},{22,14},{48,40},{50,42},{52,44},{54,46},{80... | collective-permute-start | bytes 6291464 | tf_op jit(solution)/shard_map/cond/branch_4_fun/ppermute | solution.py:370
  23.8 16.0 %collective-permute-start.30 = (bf16[16,128,256]{2,1,0:T(8,128)(2,1)}, bf16[16,128,256]{2,1,0:T(8,128)(2,1)S(1)}, u32[]{:S(2)}, u32[]{:S(2)}) collective-permute-start(bf16[16,128,256]{2,1,0:T(8,128)(2,1)} %collective-permute-done.28), channel_id=1, source_target_pairs={{24,0},{26,2},{28,4},{30,6},{56,32},{58,34},{60,36},{62,38},{88,64... | collective-permute-start | bytes 3145736 | tf_op jit(solution)/shard_map/cond/branch_4_fun/ppermute | solution.py:370
  24.6 15.3 %collective-permute-start.31 = (bf16[16,128,256]{2,1,0:T(8,128)(2,1)}, bf16[16,128,256]{2,1,0:T(8,128)(2,1)}, u32[]{:S(2)}, u32[]{:S(2)}) collective-permute-start(bf16[16,128,256]{2,1,0:T(8,128)(2,1)} %collective-permute-done.29), channel_id=1, source_target_pairs={{8,0},{10,2},{12,4},{14,6},{40,32},{42,34},{44,36},{46,38},{72,64}... | collective-permute-start | bytes 3145736 | tf_op jit(solution)/shard_map/cond/branch_4_fun/ppermute | solution.py:370
  26.2 41.7 %all-to-all-start.4 = ((bf16[64,64,128]{2,1,0:T(8,128)(2,1)}), bf16[64,64,128]{2,1,0:T(8,128)(2,1)}, u32[]{:S(2)}, u32[]{:S(2)}) async-start(bf16[64,64,128]{2,1,0:T(8,128)(2,1)} %branch_4_fun.3), calls=%async_computation.4 | async-start | bytes 2097152 | tf_op jit(solution)/shard_map/cond/branch_4_fun/all_to_all | solution.py:375
  39.8 1.0 copy-start.6
  43.5 12.7 %collective-permute-start.34 = (bf16[32,64,256]{2,1,0:T(8,128)(2,1)}, bf16[32,64,256]{2,1,0:T(8,128)(2,1)S(1)}, u32[]{:S(2)}, u32[]{:S(2)}) collective-permute-start(bf16[32,64,256]{2,1,0:T(8,128)(2,1)} %branch_4_fun.4), channel_id=1, source_target_pairs={{0,1},{2,3},{4,5},{6,7},{8,9},{10,11},{12,13},{14,15},{16,17},{18,... | collective-permute-start | bytes 3145736 | tf_op jit(solution)/shard_map/cond/branch_4_fun/ppermute | solution.py:380
  56.2 1.0 copy-start.14
  67.9 53.0 %all-to-all-start.8 = ((bf16[64,64,128]{2,1,0:T(8,128)(2,1)}), bf16[64,64,128]{2,1,0:T(8,128)(2,1)S(1)}, u32[]{:S(2)}, u32[]{:S(2)}) async-start(bf16[64,64,128]{2,1,0:T(8,128)(2,1)} %get-tuple-element.225), calls=%async_computation.8 | async-start | bytes 2097152 | tf_op jit(solution)/shard_map/all_to_all | solution.py:402
  77.8 29.7 %collective-permute-start.58 = (bf16[64,16,128]{2,1,0:T(8,128)(2,1)S(1)}, bf16[64,16,128]{2,1,0:T(8,128)(2,1)S(1)}, u32[]{:S(2)}, u32[]{:S(2)}) collective-permute-start(bf16[64,16,128]{2,1,0:T(8,128)(2,1)S(1)} %get-tuple-element.227), channel_id=1, source_target_pairs={{0,24},{8,0},{16,8},{24,16},{1,25},{9,1},{17,9},{25,17},{2,26},{10... | collective-permute-start | bytes 786440 | tf_op jit(solution)/shard_map/ppermute | solution.py:401
  94.2 21.2 %collective-permute-start.57 = (bf16[64,16,128]{2,1,0:T(8,128)(2,1)S(1)}, bf16[64,16,128]{2,1,0:T(8,128)(2,1)S(1)}, u32[]{:S(2)}, u32[]{:S(2)}) collective-permute-start(bf16[64,16,128]{2,1,0:T(8,128)(2,1)S(1)} %get-tuple-element.228), channel_id=1, source_target_pairs={{0,16},{8,24},{16,0},{24,8},{1,17},{9,25},{17,1},{25,9},{2,18},{10... | collective-permute-start | bytes 786440 | tf_op jit(solution)/shard_map/ppermute | solution.py:401
  106.1 14.8 %collective-permute-start.56 = (bf16[64,16,128]{2,1,0:T(8,128)(2,1)S(1)}, bf16[64,16,128]{2,1,0:T(8,128)(2,1)S(1)}, u32[]{:S(2)}, u32[]{:S(2)}) collective-permute-start(bf16[64,16,128]{2,1,0:T(8,128)(2,1)S(1)} %get-tuple-element.229), channel_id=1, source_target_pairs={{0,8},{8,16},{16,24},{24,0},{1,9},{9,17},{17,25},{25,1},{2,10},{10... | collective-permute-start | bytes 786440 | tf_op jit(solution)/shard_map/ppermute | solution.py:401
  107.4 13.5 %copy-start.18 = (bf16[64,16,128]{2,1,0:T(8,128)(2,1)}, bf16[64,16,128]{2,1,0:T(8,128)(2,1)S(1)}, u32[]{:S(2)}) copy-start(bf16[64,16,128]{2,1,0:T(8,128)(2,1)S(1)} %collective-permute-done.58.refs_3_) | copy-start | bytes 786436
  115.4 5.5 %copy-start.19 = (bf16[64,16,128]{2,1,0:T(8,128)(2,1)}, bf16[64,16,128]{2,1,0:T(8,128)(2,1)S(1)}, u32[]{:S(2)}) copy-start(bf16[64,16,128]{2,1,0:T(8,128)(2,1)S(1)} %collective-permute-done.57.refs_2_) | copy-start | bytes 786436
  120.9 0.7 copy-start.20
  120.9 1.1 copy-start.1

commit v2 on v1

--- a/solution.py
+++ b/solution.py
@@ -29,37 +29,40 @@
     return re * factor, im * factor
 
 
-def source_kernel(place, src_ref, far_low, far_high, up, down, own, held):
-    x = place[0]
+def source_kernel(place, src_ref, far_low, far_high, up, down, own):
     step, steps = pl.program_id(0), pl.num_programs(0)
-    data = src_ref[...].astype(F32)
-    re, im = (
-        jnp.concatenate(
-            [part[:, w * 16 + k * 8 : w * 16 + k * 8 + 8] for k in range(2) for w in range(8)],
-            axis=1,
-        )
-        for part in whiten_parts(data[..., :HALF], data[..., HALF:])
-    )
+
+    def part(start):
+        return src_ref[:, :, pl.ds(start, 128)].astype(F32)
+
+    total = None
     for q in range(4):
-        lanes = slice(q * 128, q * 128 + 128)
-        held[q, :, :, :128] = re[..., lanes].astype(BF16)
-        held[q, :, :, 128:] = im[..., lanes].astype(BF16)
-    own[...] = held[x]
-    up[...] = held[lax.rem(x + 1, 4)]
-    down[...] = held[lax.rem(x + 3, 4)]
-
-    @pl.when(step < steps // 2)
-    def _():
-        far_low[...] = held[lax.rem(x + 2, 4)]
-
-    @pl.when(step >= steps // 2)
-    def _():
-        far_high[...] = held[lax.rem(x + 2, 4)]
+        re, im = part(q * 128), part(HALF + q * 128)
+        power = re * re + im * im
+        total = power if total is None else total + power
+    level = 0.1 * (jnp.sum(total, axis=-1, keepdims=True) / HALF) + 1e-06
+
+    def emit(ahead, out):
+        start = lax.rem(place[0] + ahead, 4) * 128
+        re = part(pl.multiple_of(start, 128))
+        im = part(pl.multiple_of(HALF + start, 128))
+        factor = lax.rsqrt(re * re + im * im + level)
+        for i, value in enumerate((re * factor, im * factor)):
+            rows = [
+                value[:, w * 16 + k * 8 : w * 16 + k * 8 + 8] for k in range(2) for w in range(8)
+            ]
+            out[:, :, i * 128 : i * 128 + 128] = jnp.concatenate(rows, axis=1).astype(BF16)
+
+    emit(0, own)
+    emit(1, up)
+    emit(3, down)
+    pl.when(step < steps // 2)(functools.partial(emit, 2, far_low))
+    pl.when(step >= steps // 2)(functools.partial(emit, 2, far_high))
 
 
 def source_pieces(src, place):
     windows, sources, _ = src.shape
-    block = 4
+    block = 8
     steps = windows // block
     part = jax.ShapeDtypeStruct((windows // 2, sources, 256), BF16)
     piece = jax.ShapeDtypeStruct((windows, sources, 256), BF16)
@@ -75,7 +78,6 @@
             grid=(steps,),
             in_specs=[pl.BlockSpec((block, sources, LAGS), lambda i, p: (i, 0, 0))],
             out_specs=[low, high] + [plain] * 3,
-            scratch_shapes=[pltpu.VMEM((4,) + shape, BF16)],
         ),
         compiler_params=pltpu.CompilerParams(vmem_limit_bytes=VMEM),
         cost_estimate=pl.CostEstimate(
@@ -115,7 +117,6 @@
 
     @pl.loop(0, 4)
     def _(q):
-        ahead = lax.rem(q + 4 - place[0], 4)
         for c in range(0, chans, 2):
             pair = turn_pair(
                 *(
@@ -125,24 +126,24 @@
                 )
             )
             for i in range(2):
-                turned[pl.ds(ahead * chans + c + i, 64, stride=4 * chans), :] = pair[i]
+                turned[pl.ds(q * 64 * chans + c + i, 64, stride=chans), :] = pair[i]
 
     @pl.loop(0, 8)
     def _(j):
         rows = turned[pl.ds(pl.multiple_of(j * 32 * chans, 32 * chans), 32 * chans), :]
-        out_ref[pl.ds(j * 8, 8)] = rows.reshape(8, 4 * chans, 128).astype(BF16)
+        out_ref[pl.ds(j * 32, 32)] = rows.reshape(32, chans, 128).astype(BF16)
 
 
 def receiver_blocks(rcv, place, bad):
     windows, chans, _ = rcv.shape
     return pl.pallas_call(
         receiver_kernel,
-        out_shape=jax.ShapeDtypeStruct((64, 4 * chans, 128), BF16),
+        out_shape=jax.ShapeDtypeStruct((256, chans, 128), BF16),
         grid_spec=pltpu.PrefetchScalarGridSpec(
             num_scalar_prefetch=2,
             grid=(1,),
             in_specs=[pl.BlockSpec(rcv.shape, lambda i, p, b: (0, 0, 0))],
-            out_specs=pl.BlockSpec((64, 4 * chans, 128), lambda i, p, b: (0, 0, 0)),
+            out_specs=pl.BlockSpec((256, chans, 128), lambda i, p, b: (0, 0, 0)),
             scratch_shapes=[
                 pltpu.VMEM((8, windows * chans, 128), F32),
                 pltpu.VMEM((256 * chans, 128), F32),
@@ -258,8 +259,7 @@
     )(place, *pieces, shared)
 
 
-def cross_kernel(place, src_ref, *refs):
-    rcv_refs, out_ref, left = refs[:4], refs[4], refs[5]
+def cross_kernel(place, src_ref, rcv_ref, out_ref, left):
     row = lax.broadcasted_iota(jnp.int32, (512, 256), 0)
     col = lax.broadcasted_iota(jnp.int32, (512, 256), 1)
     wanted = ((row // 2) % 2) * 128 + (row % 2) * 64 + row // 8
@@ -277,10 +277,8 @@
         rows = jnp.dot(spread, both, preferred_element_type=F32)
         left[:, win * 128 : win * 128 + 128] = jnp.where(used, rows, 0.0).astype(BF16)
     group = lax.broadcasted_iota(jnp.int32, (64, 128), 1) // 16
-    for ahead in range(4):
-        right = jnp.concatenate(
-            [rcv_refs[ahead][w * 8 : w * 8 + 8].reshape(128, 128) for w in range(8)], axis=1
-        )
+    for x in range(4):
+        right = jnp.concatenate([rcv_ref[x * 8 + win] for win in range(8)], axis=1)
         sums = lax.dot_general(
             left[...], right, (((1,), (1,)), ((), ())), preferred_element_type=F32
         )
@@ -293,24 +291,24 @@
                 a, b = held[s], held[s + bit]
                 held[s] = jnp.where(low, a, pltpu.roll(b, 16 * bit, axis=1))
                 held[s + bit] = jnp.where(low, pltpu.roll(a, 128 - 16 * bit, axis=1), b)
-        first = lax.rem(place[0] + 4 - ahead, 4) * 64
         for g in range(8):
-            out_ref[pl.ds(first + g * 8, 8)] = held[g].reshape(8, 8, 128).astype(BF16)
-
-
-def cross_sums(place, src, rcvs):
+            first = x * 64 + g * 8
+            out_ref[first : first + 8] = held[g].reshape(8, 8, 128).astype(BF16)
+
+
+def cross_sums(place, src, rcv):
     return pl.pallas_call(
         cross_kernel,
         out_shape=jax.ShapeDtypeStruct((256, 8, 128), BF16),
         grid_spec=pltpu.PrefetchScalarGridSpec(
             num_scalar_prefetch=1,
             grid=(1,),
-            in_specs=[pl.BlockSpec(a.shape, lambda i, p: (0, 0, 0)) for a in (src, *rcvs)],
+            in_specs=[pl.BlockSpec(a.shape, lambda i, p: (0, 0, 0)) for a in (src, rcv)],
             out_specs=pl.BlockSpec((256, 8, 128), lambda i, p: (0, 0, 0)),
             scratch_shapes=[pltpu.VMEM((512, 1024), BF16)],
         ),
         compiler_params=pltpu.CompilerParams(vmem_limit_bytes=VMEM),
-    )(place, src, *rcvs)
+    )(place, src, rcv)
 
 
 def lag_kernel(cross_ref, high_ref, low_ref, out_ref, wide, sums):
@@ -332,13 +330,13 @@
     return pl.pallas_call(
         lag_kernel,
         out_shape=jax.ShapeDtypeStruct((256, LAGS), F32),
-        grid=(4,),
+        grid=(2,),
         in_specs=[
             pl.BlockSpec((256, 8, 128), lambda i: (0, 0, 0)),
-            pl.BlockSpec((1024, 256), lambda i: (0, i)),
-            pl.BlockSpec((1024, 256), lambda i: (0, i)),
+            pl.BlockSpec((1024, 512), lambda i: (0, i)),
+            pl.BlockSpec((1024, 512), lambda i: (0, i)),
         ],
-        out_specs=pl.BlockSpec((256, 256), lambda i: (0, i)),
+        out_specs=pl.BlockSpec((256, 512), lambda i: (0, i)),
         scratch_shapes=[pltpu.VMEM((2048, 128), F32), pltpu.VMEM((256, 1024), BF16)],
         compiler_params=pltpu.CompilerParams(vmem_limit_bytes=VMEM),
     )(cross, high, low)
@@ -372,7 +370,7 @@
     far_low, far_high = hop(far_low, x, 1), hop(far_high, x, -1)
     up, down = hop(up, x, 1), hop(down, x, -1)
     blocks = receiver_blocks(receiver_spectra, place, bad_channels)
-    rcv_at = lax.all_to_all(blocks, ("y", "zl", "zh", "core"), 0, 0, tiled=True)
+    rcv_at = lax.all_to_all(blocks, ("x", "y", "zl", "zh", "core"), 0, 0, tiled=True)
     far_low, far_high, _ = lax.optimization_barrier((far_low, far_high, blocks))
     far_low, far_high = hop(far_low, x + 1, 1), hop(far_high, x - 1, -1)
     pieces = (far_low, far_high, up, down, own)
@@ -395,12 +393,8 @@
         bad_channels,
         place,
     )
-    chans = rcv_at.shape[1] // 4
-    rcvs = [rcv_at[:, i * chans : i * chans + chans] for i in range(4)]
-    for i in (2, 1, 3):
-        rcvs[i] = lax.ppermute(rcvs[i], "x", [(j, (j + i) % 4) for j in range(4)])
     src_at = lax.all_to_all(src_blocks, ("y", "zl", "zh", "core"), 0, 0, tiled=True)
-    sums = cross_sums(place, src_at, rcvs)
+    sums = cross_sums(place, src_at, rcv_at.reshape(32, 128, 128))
     mine = lax.all_to_all(sums, ("x", "zh", "core", "y", "zl"), 0, 0, tiled=True)
     high, low = inverse_table()
     return to_lags(mine, high, low).reshape(16, 16, LAGS)

time: 165 us -> 152 us (0.921); the launches traced: 165 us -> 150 us
  starting transfers between devices: 62 us -> 28.5 us
  blocking collectives: 33 us -> 62.8 us
  local copies, waits for them, and re-layouts: 5.13 us -> 0.1 us
  Pallas kernels: 35.1 us -> 31.5 us
  waiting for transfers between devices: 28.9 us -> 26.4 us
    all_to_all x0 -> x1, blocking collectives: none -> 33.6 us  [on_device(): lax.all_to_all(src_blocks, ('y', 'zl', 'zh', 'core'), 0, 0, tiled=True)]
    ppermute x3 -> x0, starting transfers between devices: 29.7 us -> none  [on_device(): rcvs[i] = lax.ppermute(rcvs[i], 'x', [(j, (j + i) % 4) for j in range(4)])]
    ppermute x3 -> x0, waiting for transfers between devices: 13.5 us -> none  [on_device(): rcvs[i] = lax.ppermute(rcvs[i], 'x', [(j, (j + i) % 4) for j in range(4)])]
    all_to_all x2 -> x1, waiting for transfers between devices: 4.08 us -> 14.8 us  [exchange(): lax.all_to_all(blocks, ('x', 'y', 'zl', 'zh', 'core'), 0, 0, tiled=True)]
    ppermute x6, waiting for transfers between devices: 0.02 us -> 10.1 us  [hop(): return lax.ppermute(piece, ('x', 'core'), [pair])]
    ppermute x1, waiting for transfers between devices: 11.4 us -> 1.6 us  [exchange(): shared = lax.ppermute(share(other, place, pieces), 'core', [(core, other)])]
    all_to_all x2 -> x1, starting transfers between devices: 21.3 us -> 16.8 us  [exchange(): lax.all_to_all(blocks, ('x', 'y', 'zl', 'zh', 'core'), 0, 0, tiled=True)]
    all_to_all x1, blocking collectives: 33 us -> 29.2 us  [on_device(): lax.all_to_all(sums, ('x', 'zh', 'core', 'y', 'zl'), 0, 0, tiled=True)]
  transfers between devices with their start and end apart: 12 -> 8, of which waited for: 4 -> 4; matrix products, arithmetic and copies ran while one was open for 1% -> 0% of each run, Pallas kernels for 9% -> 9%
where the time goes in v2:
time: 152 us; the launch traced here: 150 us
  blocking collectives  62.8 us (41%)
  Pallas kernels  31.5 us (21%)
  starting transfers between devices  28.5 us (19%)
  waiting for transfers between devices  26.4 us (17%)
    all_to_all x1, blocking collectives, on_device(): lax.all_to_all(src_blocks, ('y', 'zl', 'zh', 'core'), 0, 0, tiled=True)  33.6 us
    all_to_all x1, blocking collectives, on_device(): lax.all_to_all(sums, ('x', 'zh', 'core', 'y', 'zl'), 0, 0, tiled=True)  29.2 us
    all_to_all x1, starting transfers between devices, exchange(): lax.all_to_all(blocks, ('x', 'y', 'zl', 'zh', 'core'), 0, 0, tiled=True)  16.8 us
    all_to_all x1, waiting for transfers between devices, exchange(): lax.all_to_all(blocks, ('x', 'y', 'zl', 'zh', 'core'), 0, 0, tiled=True)  14.8 us
    ppermute x6, waiting for transfers between devices, hop(): return lax.ppermute(piece, ('x', 'core'), [pair])  10.1 us
    pallas_call x1, Pallas kernels, source_pieces(): pl.pallas_call(source_kernel, out_shape=[part] * 2 + [piece] * 3, grid_sp...  9.46 us
    ppermute x6, starting transfers between devices, hop(): return lax.ppermute(piece, ('x', 'core'), [pair])  9.38 us
    pallas_call x1, Pallas kernels, turn_source(): pl.pallas_call(functools.partial(turn_kernel, holder_core), out_shape=jax...  5.61 us
  transfers between devices with their start and end apart: 8, of which 4 were waited for; matrix products, arithmetic and copies ran while one was open for 0% of the time, Pallas kernels for 9%

profile of v2, /device:TPU:1, one launch (start us, length us, event | category | flops | bytes accessed | tf_op | source)
XLA Modules:
  0.0 150.3 jit_solution(15478990146602652995)
XLA Ops:
  0.7 0.1 stack.23.place
  0.8 0.0 copy-start
  0.8 0.0 copy-start.9
  0.8 9.5 %shard_map.64 = (bf16[16,128,256]{2,1,0:T(8,128)(2,1)}, bf16[16,128,256]{2,1,0:T(8,128)(2,1)}, bf16[32,128,256]{2,1,0:T(8,128)(2,1)}, bf16[32,128,256]{2,1,0:T(8,128)(2,1)}, bf16[32,128,256]{2,1,0:T(8,128)(2,1)S(1)}) custom-call(s32[5]{0:T(128)S(1)} %stack.23.place, bf16[32,128,1024]{2,1,0:T(8,128)(2,1)} %src_ref.1), custom_call_target="tpu_custom_call" | custom-call | flops 40000000 | bytes 16777216 | tf_op jit(solution)/shard_map/pallas_call | solution.py:73
  10.3 0.0 copy-done
  10.3 0.0 copy-done.9
  10.3 68.1 %conditional.1 = (bf16[64,64,128]{2,1,0:T(8,128)(2,1)S(1)}, bf16[32,128,128]{2,1,0:T(8,128)(2,1)}) conditional(s32[]{:T(128)} %clamp.3, (bf16[16,128,256]{2,1,0:T(8,128)(2,1)}, bf16[16,128,256]{2,1,0:T(8,128)(2,1)}, s32[5]{0:T(128)S(1)}, s32[64]{0:T(128)S(1)}, bf16[32,16,1024]{2,1,0:T(8,128)(2,1)S(1)}, ...), branch_computations={%region_0.1_spmd, %region_1.2_spmd, %region_2.3_spmd, %region_3.4_... | conditional | flops 20000000 | bytes 47186276 | solution.py:388
  10.6 1.3 collective-permute-start.49
  11.9 1.7 %collective-permute-start.50 = (bf16[16,128,256]{2,1,0:T(8,128)(2,1)}, bf16[16,128,256]{2,1,0:T(8,128)(2,1)}, u32[]{:S(2)}, u32[]{:S(2)}) collective-permute-start(bf16[16,128,256]{2,1,0:T(8,128)(2,1)} %get-tuple-element.206), channel_id=1, source_target_pairs={{25,17},{27,19},{29,21},{31,23},{57,49},{59,51},{61,53},{63,55},{8... | collective-permute-start | bytes 3145736 | tf_op jit(solution)/shard_map/cond/branch_7_fun/ppermute | solution.py:368
  13.5 1.3 collective-permute-start.53
  14.8 2.1 %collective-permute-start.54 = (bf16[32,128,256]{2,1,0:T(8,128)(2,1)}, bf16[32,128,256]{2,1,0:T(8,128)(2,1)}, u32[]{:S(2)}, u32[]{:S(2)}) collective-permute-start(bf16[32,128,256]{2,1,0:T(8,128)(2,1)} %get-tuple-element.212), channel_id=1, source_target_pairs={{25,17},{27,19},{29,21},{31,23},{57,49},{59,51},{61,53},{63,55},{8... | collective-permute-start | bytes 6291464 | tf_op jit(solution)/shard_map/cond/branch_7_fun/ppermute | solution.py:368
  16.9 4.5 %branch_7_fun.3 = bf16[256,16,128]{2,1,0:T(8,128)(2,1)} custom-call(s32[5]{0:T(128)S(1)} %get-tuple-element.204.place, s32[64]{0:T(128)S(1)} %get-tuple-element.207.bad, bf16[32,16,1024]{2,1,0:T(8,128)(2,1)S(1)} %get-tuple-element.208.rcv_ref), custom_call_target="tpu_custom_call" | custom-call | flops 20000000 | bytes 2097152 | tf_op jit(solution)/shard_map/cond/branch_7_fun/pallas_call | solution.py:139
  21.4 6.2 %collective-permute-done.49 = bf16[16,128,256]{2,1,0:T(8,128)(2,1)} collective-permute-done((bf16[16,128,256]{2,1,0:T(8,128)(2,1)}, bf16[16,128,256]{2,1,0:T(8,128)(2,1)}, u32[]{:S(2)}, u32[]{:S(2)}) %collective-permute-start.49) | collective-permute-done | bytes 1048608 | tf_op jit(solution)/shard_map/cond/branch_7_fun/ppermute | solution.py:368
  27.6 0.0 collective-permute-done.50
  27.6 1.3 collective-permute-start.51
  29.0 1.7 %collective-permute-start.52 = (bf16[16,128,256]{2,1,0:T(8,128)(2,1)}, bf16[16,128,256]{2,1,0:T(8,128)(2,1)}, u32[]{:S(2)}, u32[]{:S(2)}) collective-permute-start(bf16[16,128,256]{2,1,0:T(8,128)(2,1)} %collective-permute-done.50), channel_id=1, source_target_pairs={{17,9},{19,11},{21,13},{23,15},{49,41},{51,43},{53,45},{55,47},{81... | collective-permute-start | bytes 3145736 | tf_op jit(solution)/shard_map/cond/branch_7_fun/ppermute | solution.py:368
  30.7 16.8 %all-to-all-start.7 = ((bf16[256,16,128]{2,1,0:T(8,128)(2,1)}), bf16[256,16,128]{2,1,0:T(8,128)(2,1)}, u32[]{:S(2)}, u32[]{:S(2)}) async-start(bf16[256,16,128]{2,1,0:T(8,128)(2,1)} %branch_7_fun.3), calls=%async_computation.7 | async-start | bytes 2097152 | tf_op jit(solution)/shard_map/cond/branch_7_fun/all_to_all | solution.py:373
  47.5 0.0 collective-permute-done.51.refs_0_
  47.5 0.0 copy-start.8
  47.5 0.0 collective-permute-done.52.refs_1_
  47.5 3.8 %collective-permute-done.53.refs_2_ = bf16[32,128,256]{2,1,0:T(8,128)(2,1)} collective-permute-done((bf16[32,128,256]{2,1,0:T(8,128)(2,1)}, bf16[32,128,256]{2,1,0:T(8,128)(2,1)}, u32[]{:S(2)}, u32[]{:S(2)}) %collective-permute-start.53) | collective-permute-done | bytes 2097184 | tf_op jit(solution)/shard_map/cond/branch_7_fun/ppermute | solution.py:368
  51.3 0.0 collective-permute-done.54.refs_3_
  51.3 0.0 copy-done.8
  51.3 2.8 %branch_7_fun.4 = bf16[32,64,256]{2,1,0:T(8,128)(2,1)} custom-call(s32[5]{0:T(128)S(1)} %get-tuple-element.204.place, bf16[16,128,256]{2,1,0:T(8,128)(2,1)} %copy-done.8, bf16[16,128,256]{2,1,0:T(8,128)(2,1)} %collective-permute-done.52.refs_1_, bf16[32,128,256]{2,1,0:T(8,128)(2,1)} %collective-permute-done.53.refs_2_, ...), custom_call_target="tpu_custom_call" | custom-call | tf_op jit(solution)/shard_map/cond/branch_7_fun/pallas_call | solution.py:187
  54.1 2.3 %collective-permute-start.55 = (bf16[32,64,256]{2,1,0:T(8,128)(2,1)}, bf16[32,64,256]{2,1,0:T(8,128)(2,1)}, u32[]{:S(2)}, u32[]{:S(2)}) collective-permute-start(bf16[32,64,256]{2,1,0:T(8,128)(2,1)} %branch_7_fun.4), channel_id=1, source_target_pairs={{1,0},{3,2},{5,4},{7,6},{9,8},{11,10},{13,12},{15,14},{17,16},{19,... | collective-permute-start | bytes 3145736 | tf_op jit(solution)/shard_map/cond/branch_7_fun/ppermute | solution.py:378
  56.4 1.6 %collective-permute-done.55.refs_5_ = bf16[32,64,256]{2,1,0:T(8,128)(2,1)} collective-permute-done((bf16[32,64,256]{2,1,0:T(8,128)(2,1)}, bf16[32,64,256]{2,1,0:T(8,128)(2,1)}, u32[]{:S(2)}, u32[]{:S(2)}) %collective-permute-start.55) | collective-permute-done | bytes 1048608 | tf_op jit(solution)/shard_map/cond/branch_7_fun/ppermute | solution.py:378
  58.0 5.6 %branch_7_fun.5 = bf16[64,64,128]{2,1,0:T(8,128)(2,1)S(1)} custom-call(s32[5]{0:T(128)S(1)} %get-tuple-element.204.place, bf16[16,128,256]{2,1,0:T(8,128)(2,1)} %copy-done.8, bf16[16,128,256]{2,1,0:T(8,128)(2,1)} %collective-permute-done.52.refs_1_, bf16[32,128,256]{2,1,0:T(8,128)(2,1)} %collective-permute-done.53.refs_2_, ...), custom_call_target="tpu_custom_call" | custom-call | tf_op jit(solution)/shard_map/cond/branch_7_fun/pallas_call | solution.py:243
  63.6 14.8 %all-to-all-done.7 = bf16[256,16,128]{2,1,0:T(8,128)(2,1)} async-done(((bf16[256,16,128]{2,1,0:T(8,128)(2,1)}), bf16[256,16,128]{2,1,0:T(8,128)(2,1)}, u32[]{:S(2)}, u32[]{:S(2)}) %all-to-all-start.7) | async-done | bytes 1048608 | tf_op jit(solution)/shard_map/cond/branch_7_fun/all_to_all | solution.py:373
  78.4 33.6 %all_to_all.42.src_ref = bf16[64,64,128]{2,1,0:T(8,128)(2,1)} all-to-all(bf16[64,64,128]{2,1,0:T(8,128)(2,1)S(1)} %get-tuple-element.226), channel_id=1, replica_groups=mesh['y'=4,'zl'=2,'x'=4,'zh'=4,'core'=2] {'y','zl','zh','core'}, dimensions={0} | all-to-all | bytes 2097152 | tf_op jit(solution)/shard_map/all_to_all | solution.py:396
  112.0 5.0 %shard_map.65 = bf16[256,8,128]{2,1,0:T(8,128)(2,1)} custom-call(s32[5]{0:T(128)S(1)} %stack.23.place, bf16[64,64,128]{2,1,0:T(8,128)(2,1)} %all_to_all.42.src_ref, bf16[32,128,128]{2,1,0:T(8,128)(2,1)} %get-tuple-element.227.rcv_ref), custom_call_target="tpu_custom_call" | custom-call | tf_op jit(solution)/shard_map/pallas_call | solution.py:300
  117.0 29.2 %all_to_all.43.cross_ref = bf16[256,8,128]{2,1,0:T(8,128)(2,1)} all-to-all(bf16[256,8,128]{2,1,0:T(8,128)(2,1)} %shard_map.65), channel_id=1, replica_groups=mesh['y'=4,'zl'=2,'x'=4,'zh'=4,'core'=2] {'x','zh','core','y','zl'}, dimensions={0} | all-to-all | bytes 1048576 | tf_op jit(solution)/shard_map/all_to_all | solution.py:398
  146.1 4.2 %shard_map.66 = f32[256,1024]{1,0:T(8,128)} custom-call(bf16[256,8,128]{2,1,0:T(8,128)(2,1)} %all_to_all.43.cross_ref, bf16[1024,1024]{1,0:T(8,128)(2,1)} %constant.67.clone.high_ref, bf16[1024,1024]{1,0:T(8,128)(2,1)} %constant.68.clone.low_ref), custom_call_target="tpu_custom_call" | custom-call | tf_op jit(solution)/shard_map/pallas_call | solution.py:330
Async XLA Ops:
  0.8 9.5 %copy-start = (bf16[32,16,1024]{2,1,0:T(8,128)(2,1)S(1)}, bf16[32,16,1024]{2,1,0:T(8,128)(2,1)}, u32[]{:S(2)}) copy-start(bf16[32,16,1024]{2,1,0:T(8,128)(2,1)} %param.15) | copy-start | bytes 3145732
  0.8 9.5 %copy-start.9 = (s32[64]{0:T(128)S(1)}, s32[64]{0:T(128)}, u32[]{:S(2)}) copy-start(s32[64]{0:T(128)} %param.17) | copy-start | bytes 772
  10.6 17.1 %collective-permute-start.49 = (bf16[16,128,256]{2,1,0:T(8,128)(2,1)}, bf16[16,128,256]{2,1,0:T(8,128)(2,1)}, u32[]{:S(2)}, u32[]{:S(2)}) collective-permute-start(bf16[16,128,256]{2,1,0:T(8,128)(2,1)} %get-tuple-element.205), channel_id=1, source_target_pairs={{25,1},{27,3},{29,5},{31,7},{57,33},{59,35},{61,37},{63,39},{89,65... | collective-permute-start | bytes 3145736 | tf_op jit(solution)/shard_map/cond/branch_7_fun/ppermute | solution.py:368
  11.9 15.8 %collective-permute-start.50 = (bf16[16,128,256]{2,1,0:T(8,128)(2,1)}, bf16[16,128,256]{2,1,0:T(8,128)(2,1)}, u32[]{:S(2)}, u32[]{:S(2)}) collective-permute-start(bf16[16,128,256]{2,1,0:T(8,128)(2,1)} %get-tuple-element.206), channel_id=1, source_target_pairs={{25,17},{27,19},{29,21},{31,23},{57,49},{59,51},{61,53},{63,55},{8... | collective-permute-start | bytes 3145736 | tf_op jit(solution)/shard_map/cond/branch_7_fun/ppermute | solution.py:368
  13.5 37.8 %collective-permute-start.53 = (bf16[32,128,256]{2,1,0:T(8,128)(2,1)}, bf16[32,128,256]{2,1,0:T(8,128)(2,1)}, u32[]{:S(2)}, u32[]{:S(2)}) collective-permute-start(bf16[32,128,256]{2,1,0:T(8,128)(2,1)} %get-tuple-element.211), channel_id=1, source_target_pairs={{25,1},{27,3},{29,5},{31,7},{57,33},{59,35},{61,37},{63,39},{89,65... | collective-permute-start | bytes 6291464 | tf_op jit(solution)/shard_map/cond/branch_7_fun/ppermute | solution.py:368
  14.8 36.5 %collective-permute-start.54 = (bf16[32,128,256]{2,1,0:T(8,128)(2,1)}, bf16[32,128,256]{2,1,0:T(8,128)(2,1)}, u32[]{:S(2)}, u32[]{:S(2)}) collective-permute-start(bf16[32,128,256]{2,1,0:T(8,128)(2,1)} %get-tuple-element.212), channel_id=1, source_target_pairs={{25,17},{27,19},{29,21},{31,23},{57,49},{59,51},{61,53},{63,55},{8... | collective-permute-start | bytes 6291464 | tf_op jit(solution)/shard_map/cond/branch_7_fun/ppermute | solution.py:368
  27.6 19.9 %collective-permute-start.51 = (bf16[16,128,256]{2,1,0:T(8,128)(2,1)}, bf16[16,128,256]{2,1,0:T(8,128)(2,1)S(1)}, u32[]{:S(2)}, u32[]{:S(2)}) collective-permute-start(bf16[16,128,256]{2,1,0:T(8,128)(2,1)} %collective-permute-done.49), channel_id=1, source_target_pairs={{1,9},{3,11},{5,13},{7,15},{33,41},{35,43},{37,45},{39,47},{65,73}... | collective-permute-start | bytes 3145736 | tf_op jit(solution)/shard_map/cond/branch_7_fun/ppermute | solution.py:368
  29.0 18.5 %collective-permute-start.52 = (bf16[16,128,256]{2,1,0:T(8,128)(2,1)}, bf16[16,128,256]{2,1,0:T(8,128)(2,1)}, u32[]{:S(2)}, u32[]{:S(2)}) collective-permute-start(bf16[16,128,256]{2,1,0:T(8,128)(2,1)} %collective-permute-done.50), channel_id=1, source_target_pairs={{17,9},{19,11},{21,13},{23,15},{49,41},{51,43},{53,45},{55,47},{81... | collective-permute-start | bytes 3145736 | tf_op jit(solution)/shard_map/cond/branch_7_fun/ppermute | solution.py:368
  30.7 47.7 %all-to-all-start.7 = ((bf16[256,16,128]{2,1,0:T(8,128)(2,1)}), bf16[256,16,128]{2,1,0:T(8,128)(2,1)}, u32[]{:S(2)}, u32[]{:S(2)}) async-start(bf16[256,16,128]{2,1,0:T(8,128)(2,1)} %branch_7_fun.3), calls=%async_computation.7 | async-start | bytes 2097152 | tf_op jit(solution)/shard_map/cond/branch_7_fun/all_to_all | solution.py:373
  47.5 3.8 %copy-start.8 = (bf16[16,128,256]{2,1,0:T(8,128)(2,1)}, bf16[16,128,256]{2,1,0:T(8,128)(2,1)S(1)}, u32[]{:S(2)}) copy-start(bf16[16,128,256]{2,1,0:T(8,128)(2,1)S(1)} %collective-permute-done.51.refs_0_) | copy-start | bytes 3145732 | tf_op jit(solution)/shard_map/cond
  54.1 3.9 %collective-permute-start.55 = (bf16[32,64,256]{2,1,0:T(8,128)(2,1)}, bf16[32,64,256]{2,1,0:T(8,128)(2,1)}, u32[]{:S(2)}, u32[]{:S(2)}) collective-permute-start(bf16[32,64,256]{2,1,0:T(8,128)(2,1)} %branch_7_fun.4), channel_id=1, source_target_pairs={{1,0},{3,2},{5,4},{7,6},{9,8},{11,10},{13,12},{15,14},{17,16},{19,... | collective-permute-start | bytes 3145736 | tf_op jit(solution)/shard_map/cond/branch_7_fun/ppermute | solution.py:378

commit v3 on v2

--- a/solution.py
+++ b/solution.py
@@ -103,7 +103,7 @@
     for i in range(bad.shape[0]):
         faulty = faulty | (ids == bad[i])
     keep = jnp.where(faulty, 0.0, 1.0).astype(F32)[None, :, :1]
-    group = 4
+    group = 8
 
     @pl.loop(0, windows // group)
     def _(j):
@@ -128,10 +128,10 @@
             for i in range(2):
                 turned[pl.ds(q * 64 * chans + c + i, 64, stride=chans), :] = pair[i]
 
-    @pl.loop(0, 8)
+    @pl.loop(0, 4)
     def _(j):
-        rows = turned[pl.ds(pl.multiple_of(j * 32 * chans, 32 * chans), 32 * chans), :]
-        out_ref[pl.ds(j * 32, 32)] = rows.reshape(32, chans, 128).astype(BF16)
+        rows = turned[pl.ds(pl.multiple_of(j * 64 * chans, 64 * chans), 64 * chans), :]
+        out_ref[pl.ds(j * 64, 64)] = rows.reshape(64, chans, 128).astype(BF16)
 
 
 def receiver_blocks(rcv, place, bad):
@@ -194,7 +194,7 @@
             out_specs=pl.BlockSpec((windows, 64, 256), lambda i, p: (0, 0, 0)),
             scratch_shapes=[pltpu.SemaphoreType.DMA((2,))],
         ),
-        compiler_params=pltpu.CompilerParams(vmem_limit_bytes=VMEM),
+        compiler_params=pltpu.CompilerParams(vmem_limit_bytes=VMEM // 2),
     )(place, *pieces)
 
 
@@ -255,7 +255,7 @@
                 pltpu.SemaphoreType.DMA((2,)),
             ],
         ),
-        compiler_params=pltpu.CompilerParams(vmem_limit_bytes=VMEM),
+        compiler_params=pltpu.CompilerParams(vmem_limit_bytes=VMEM // 2),
     )(place, *pieces, shared)
 
 
@@ -267,10 +267,8 @@
     lane = lax.broadcasted_iota(jnp.int32, (512, 128), 1)
     used = (lax.broadcasted_iota(jnp.int32, (512, 128), 0) // 4) % 2 == lane // 64
     is_real = lane[:128] % 64 < 32
-    zh = place[4]
     for win in range(8):
-        base = (win * 4 + zh) * 2
-        plain = jnp.concatenate([src_ref[base], src_ref[base + 1]], axis=0)
+        plain = src_ref[win, 0]
         wide = plain.astype(F32)
         turned = jnp.where(is_real, -pltpu.roll(wide, 96, axis=1), pltpu.roll(wide, 32, axis=1))
         both = jnp.concatenate([plain, turned.astype(BF16)], axis=0)
@@ -303,12 +301,15 @@
         grid_spec=pltpu.PrefetchScalarGridSpec(
             num_scalar_prefetch=1,
             grid=(1,),
-            in_specs=[pl.BlockSpec(a.shape, lambda i, p: (0, 0, 0)) for a in (src, rcv)],
+            in_specs=[
+                pl.BlockSpec((8, 1, 128, 128), lambda i, p: (0, p[4], 0, 0)),
+                pl.BlockSpec(rcv.shape, lambda i, p: (0, 0, 0)),
+            ],
             out_specs=pl.BlockSpec((256, 8, 128), lambda i, p: (0, 0, 0)),
             scratch_shapes=[pltpu.VMEM((512, 1024), BF16)],
         ),
-        compiler_params=pltpu.CompilerParams(vmem_limit_bytes=VMEM),
-    )(place, src, rcv)
+        compiler_params=pltpu.CompilerParams(vmem_limit_bytes=VMEM // 2),
+    )(place, src.reshape(8, 4, 128, 128), rcv)
 
 
 def lag_kernel(cross_ref, high_ref, low_ref, out_ref, wide, sums):

time: 152 us -> 152 us (level)
  starting transfers between devices: 28.5 us -> 32 us
  Pallas kernels: 31.5 us -> 29.6 us
    ppermute x6, starting transfers between devices: 9.38 us -> 14.4 us  [hop(): return lax.ppermute(piece, ('x', 'core'), [pair])]
    all_to_all x1, waiting for transfers between devices: 14.8 us -> 12.5 us  [exchange(): lax.all_to_all(blocks, ('x', 'y', 'zl', 'zh', 'core'), 0, 0, tiled=True)]
  transfers between devices with their start and end apart: 8 -> 8, of which waited for: 4 -> 5; matrix products, arithmetic and copies ran while one was open for 0% -> 0% of each run, Pallas kernels for 9% -> 8%
where the time goes in v3:
time: 152 us; the launch traced here: 151 us
  blocking collectives  63.4 us (42%)
  starting transfers between devices  32 us (21%)
  Pallas kernels  29.6 us (19%)
  waiting for transfers between devices  24.9 us (16%)
    all_to_all x1, blocking collectives, on_device(): lax.all_to_all(src_blocks, ('y', 'zl', 'zh', 'core'), 0, 0, tiled=True)  33.8 us
    all_to_all x1, blocking collectives, on_device(): lax.all_to_all(sums, ('x', 'zh', 'core', 'y', 'zl'), 0, 0, tiled=True)  29.6 us
    all_to_all x1, starting transfers between devices, exchange(): lax.all_to_all(blocks, ('x', 'y', 'zl', 'zh', 'core'), 0, 0, tiled=True)  16.3 us
    ppermute x6, starting transfers between devices, hop(): return lax.ppermute(piece, ('x', 'core'), [pair])  14.4 us
    all_to_all x1, waiting for transfers between devices, exchange(): lax.all_to_all(blocks, ('x', 'y', 'zl', 'zh', 'core'), 0, 0, tiled=True)  12.5 us
    ppermute x6, waiting for transfers between devices, hop(): return lax.ppermute(piece, ('x', 'core'), [pair])  10.2 us
    pallas_call x1, Pallas kernels, source_pieces(): pl.pallas_call(source_kernel, out_shape=[part] * 2 + [piece] * 3, grid_sp...  10 us
    pallas_call x1, Pallas kernels, turn_source(): pl.pallas_call(functools.partial(turn_kernel, holder_core), out_shape=jax...  5.54 us
  transfers between devices with their start and end apart: 8, of which 5 were waited for; matrix products, arithmetic and copies ran while one was open for 0% of the time, Pallas kernels for 8%

profile of v3, /device:TPU:1, one launch (start us, length us, event | category | flops | bytes accessed | tf_op | source)
XLA Modules:
  0.0 150.9 jit_solution(16203872311198149090)
XLA Ops:
  0.7 0.1 stack.23.place
  0.8 0.0 copy-start.8
  0.8 0.0 copy-start.9
  0.8 10.0 %shard_map.64 = (bf16[16,128,256]{2,1,0:T(8,128)(2,1)}, bf16[16,128,256]{2,1,0:T(8,128)(2,1)}, bf16[32,128,256]{2,1,0:T(8,128)(2,1)}, bf16[32,128,256]{2,1,0:T(8,128)(2,1)}, bf16[32,128,256]{2,1,0:T(8,128)(2,1)}) custom-call(s32[5]{0:T(128)S(1)} %stack.23.place, bf16[32,128,1024]{2,1,0:T(8,128)(2,1)} %src_ref.1), custom_call_target="tpu_custom_call" | custom-call | flops 40000000 | bytes 16777216 | tf_op jit(solution)/shard_map/pallas_call | solution.py:73
  10.8 0.0 copy-done.8
  10.8 0.0 copy-done.9
  10.8 68.6 %conditional.1 = (bf16[64,64,128]{2,1,0:T(8,128)(2,1)}, bf16[32,128,128]{2,1,0:T(8,128)(2,1)}) conditional(s32[]{:T(128)} %clamp.3, (bf16[16,128,256]{2,1,0:T(8,128)(2,1)}, bf16[16,128,256]{2,1,0:T(8,128)(2,1)}, s32[5]{0:T(128)S(1)}, s32[64]{0:T(128)S(1)}, bf16[32,16,1024]{2,1,0:T(8,128)(2,1)S(1)}, ...), branch_computations={%region_0.1_spmd, %region_1.2_spmd, %region_2.3_spmd, %region_3.4_... | conditional | flops 20000000 | bytes 51380580 | solution.py:389
  10.9 5.0 %collective-permute-start.7 = (bf16[16,128,256]{2,1,0:T(8,128)(2,1)}, bf16[16,128,256]{2,1,0:T(8,128)(2,1)}, u32[]{:S(2)}, u32[]{:S(2)}) collective-permute-start(bf16[16,128,256]{2,1,0:T(8,128)(2,1)} %get-tuple-element.145), channel_id=1, source_target_pairs={{1,9},{3,11},{5,13},{7,15},{33,41},{35,43},{37,45},{39,47},{65,73}... | collective-permute-start | bytes 3145736 | tf_op jit(solution)/shard_map/cond/branch_1_fun/ppermute | solution.py:369
  15.9 2.9 %collective-permute-start.8 = (bf16[16,128,256]{2,1,0:T(8,128)(2,1)}, bf16[16,128,256]{2,1,0:T(8,128)(2,1)}, u32[]{:S(2)}, u32[]{:S(2)}) collective-permute-start(bf16[16,128,256]{2,1,0:T(8,128)(2,1)} %get-tuple-element.146), channel_id=1, source_target_pairs={{1,25},{3,27},{5,29},{7,31},{33,57},{35,59},{37,61},{39,63},{65,89... | collective-permute-start | bytes 3145736 | tf_op jit(solution)/shard_map/cond/branch_1_fun/ppermute | solution.py:369
  18.8 1.4 collective-permute-start.11
  20.2 2.7 %collective-permute-start.12 = (bf16[32,128,256]{2,1,0:T(8,128)(2,1)}, bf16[32,128,256]{2,1,0:T(8,128)(2,1)}, u32[]{:S(2)}, u32[]{:S(2)}) collective-permute-start(bf16[32,128,256]{2,1,0:T(8,128)(2,1)} %get-tuple-element.152), channel_id=1, source_target_pairs={{1,25},{3,27},{5,29},{7,31},{33,57},{35,59},{37,61},{39,63},{65,89... | collective-permute-start | bytes 6291464 | tf_op jit(solution)/shard_map/cond/branch_1_fun/ppermute | solution.py:369
  22.9 4.1 %branch_1_fun.3 = bf16[256,16,128]{2,1,0:T(8,128)(2,1)} custom-call(s32[5]{0:T(128)S(1)} %get-tuple-element.144.place, s32[64]{0:T(128)S(1)} %get-tuple-element.147.bad, bf16[32,16,1024]{2,1,0:T(8,128)(2,1)S(1)} %get-tuple-element.148.rcv_ref), custom_call_target="tpu_custom_call" | custom-call | flops 20000000 | bytes 2097152 | tf_op jit(solution)/shard_map/cond/branch_1_fun/pallas_call | solution.py:139
  27.0 0.0 collective-permute-done.7
  27.0 2.8 %collective-permute-done.8 = bf16[16,128,256]{2,1,0:T(8,128)(2,1)} collective-permute-done((bf16[16,128,256]{2,1,0:T(8,128)(2,1)}, bf16[16,128,256]{2,1,0:T(8,128)(2,1)}, u32[]{:S(2)}, u32[]{:S(2)}) %collective-permute-start.8) | collective-permute-done | bytes 1048608 | tf_op jit(solution)/shard_map/cond/branch_1_fun/ppermute | solution.py:369
  29.8 0.7 collective-permute-start.9
  30.5 1.7 %collective-permute-start.10 = (bf16[16,128,256]{2,1,0:T(8,128)(2,1)}, bf16[16,128,256]{2,1,0:T(8,128)(2,1)}, u32[]{:S(2)}, u32[]{:S(2)}) collective-permute-start(bf16[16,128,256]{2,1,0:T(8,128)(2,1)} %collective-permute-done.8), channel_id=1, source_target_pairs={{25,17},{27,19},{29,21},{31,23},{57,49},{59,51},{61,53},{63,55},{8... | collective-permute-start | bytes 3145736 | tf_op jit(solution)/shard_map/cond/branch_1_fun/ppermute | solution.py:369
  32.2 16.3 %all-to-all-start.1 = ((bf16[256,16,128]{2,1,0:T(8,128)(2,1)}), bf16[256,16,128]{2,1,0:T(8,128)(2,1)}, u32[]{:S(2)}, u32[]{:S(2)}) async-start(bf16[256,16,128]{2,1,0:T(8,128)(2,1)} %branch_1_fun.3), calls=%async_computation.1 | async-start | bytes 2097152 | tf_op jit(solution)/shard_map/cond/branch_1_fun/all_to_all | solution.py:374
  48.5 0.0 collective-permute-done.9.refs_0_
  48.5 0.0 collective-permute-done.10.refs_1_
  48.5 1.5 collective-permute-done.11.refs_2_
  50.0 5.9 %collective-permute-done.12.refs_3_ = bf16[32,128,256]{2,1,0:T(8,128)(2,1)} collective-permute-done((bf16[32,128,256]{2,1,0:T(8,128)(2,1)}, bf16[32,128,256]{2,1,0:T(8,128)(2,1)}, u32[]{:S(2)}, u32[]{:S(2)}) %collective-permute-start.12) | collective-permute-done | bytes 2097184 | tf_op jit(solution)/shard_map/cond/branch_1_fun/ppermute | solution.py:369
  55.9 0.0 copy-start.1
  55.9 1.9 %branch_1_fun.4 = bf16[32,64,256]{2,1,0:T(8,128)(2,1)S(1)} custom-call(s32[5]{0:T(128)S(1)} %get-tuple-element.144.place, bf16[16,128,256]{2,1,0:T(8,128)(2,1)S(1)} %collective-permute-done.9.refs_0_, bf16[16,128,256]{2,1,0:T(8,128)(2,1)} %collective-permute-done.10.refs_1_, bf16[32,128,256]{2,1,0:T(8,128)(2,1)S(1)} %collective-permute-done.11.refs_2_, ...), custom_call_target="tpu_custom_call" | custom-call | tf_op jit(solution)/shard_map/cond/branch_1_fun/pallas_call | solution.py:187
  57.8 1.4 collective-permute-start.13
  59.2 2.2 %collective-permute-done.13.refs_5_ = bf16[32,64,256]{2,1,0:T(8,128)(2,1)S(1)} collective-permute-done((bf16[32,64,256]{2,1,0:T(8,128)(2,1)S(1)}, bf16[32,64,256]{2,1,0:T(8,128)(2,1)S(1)}, u32[]{:S(2)}, u32[]{:S(2)}) %collective-permute-start.13) | collective-permute-done | bytes 1048608 | tf_op jit(solution)/shard_map/cond/branch_1_fun/ppermute | solution.py:379
  61.4 0.0 copy-done.1
  61.4 5.5 %branch_1_fun.5 = bf16[64,64,128]{2,1,0:T(8,128)(2,1)} custom-call(s32[5]{0:T(128)S(1)} %get-tuple-element.144.place, bf16[16,128,256]{2,1,0:T(8,128)(2,1)S(1)} %collective-permute-done.9.refs_0_, bf16[16,128,256]{2,1,0:T(8,128)(2,1)} %collective-permute-done.10.refs_1_, bf16[32,128,256]{2,1,0:T(8,128)(2,1)S(1)} %collective-permute-done.11.refs_2_, ...), custom_call_target="tpu_custom_call" | custom-call | tf_op jit(solution)/shard_map/cond/branch_1_fun/pallas_call | solution.py:243
  66.9 12.5 %all-to-all-done.1 = bf16[256,16,128]{2,1,0:T(8,128)(2,1)} async-done(((bf16[256,16,128]{2,1,0:T(8,128)(2,1)}), bf16[256,16,128]{2,1,0:T(8,128)(2,1)}, u32[]{:S(2)}, u32[]{:S(2)}) %all-to-all-start.1) | async-done | bytes 1048608 | tf_op jit(solution)/shard_map/cond/branch_1_fun/all_to_all | solution.py:374
  79.4 33.8 %all_to_all.42 = bf16[64,64,128]{2,1,0:T(8,128)(2,1)S(1)} all-to-all(bf16[64,64,128]{2,1,0:T(8,128)(2,1)} %get-tuple-element.226), channel_id=1, replica_groups=mesh['y'=4,'zl'=2,'x'=4,'zh'=4,'core'=2] {'y','zl','zh','core'}, dimensions={0} | all-to-all | bytes 2097152 | tf_op jit(solution)/shard_map/all_to_all | solution.py:397
  113.2 3.9 %shard_map.65 = bf16[256,8,128]{2,1,0:T(8,128)(2,1)S(1)} custom-call(s32[5]{0:T(128)S(1)} %stack.23.place, bf16[8,4,128,128]{3,2,1,0:T(8,128)(2,1)S(1)} %bitcast.20, bf16[32,128,128]{2,1,0:T(8,128)(2,1)} %get-tuple-element.227.rcv_ref), custom_call_target="tpu_custom_call" | custom-call | tf_op jit(solution)/shard_map/pallas_call | solution.py:298
  117.1 29.6 %all_to_all.43.cross_ref = bf16[256,8,128]{2,1,0:T(8,128)(2,1)} all-to-all(bf16[256,8,128]{2,1,0:T(8,128)(2,1)S(1)} %shard_map.65), channel_id=1, replica_groups=mesh['y'=4,'zl'=2,'x'=4,'zh'=4,'core'=2] {'x','zh','core','y','zl'}, dimensions={0} | all-to-all | bytes 1048576 | tf_op jit(solution)/shard_map/all_to_all | solution.py:399
  146.7 4.2 %shard_map.66 = f32[256,1024]{1,0:T(8,128)} custom-call(bf16[256,8,128]{2,1,0:T(8,128)(2,1)} %all_to_all.43.cross_ref, bf16[1024,1024]{1,0:T(8,128)(2,1)} %constant.67.clone.high_ref, bf16[1024,1024]{1,0:T(8,128)(2,1)} %constant.68.clone.low_ref), custom_call_target="tpu_custom_call" | custom-call | tf_op jit(solution)/shard_map/pallas_call | solution.py:331
Async XLA Ops:
  0.8 10.0 %copy-start.8 = (bf16[32,16,1024]{2,1,0:T(8,128)(2,1)S(1)}, bf16[32,16,1024]{2,1,0:T(8,128)(2,1)}, u32[]{:S(2)}) copy-start(bf16[32,16,1024]{2,1,0:T(8,128)(2,1)} %param.15) | copy-start | bytes 3145732
  0.8 10.0 %copy-start.9 = (s32[64]{0:T(128)S(1)}, s32[64]{0:T(128)}, u32[]{:S(2)}) copy-start(s32[64]{0:T(128)} %param.17) | copy-start | bytes 772
  10.9 16.1 %collective-permute-start.7 = (bf16[16,128,256]{2,1,0:T(8,128)(2,1)}, bf16[16,128,256]{2,1,0:T(8,128)(2,1)}, u32[]{:S(2)}, u32[]{:S(2)}) collective-permute-start(bf16[16,128,256]{2,1,0:T(8,128)(2,1)} %get-tuple-element.145), channel_id=1, source_target_pairs={{1,9},{3,11},{5,13},{7,15},{33,41},{35,43},{37,45},{39,47},{65,73}... | collective-permute-start | bytes 3145736 | tf_op jit(solution)/shard_map/cond/branch_1_fun/ppermute | solution.py:369
  15.9 14.0 %collective-permute-start.8 = (bf16[16,128,256]{2,1,0:T(8,128)(2,1)}, bf16[16,128,256]{2,1,0:T(8,128)(2,1)}, u32[]{:S(2)}, u32[]{:S(2)}) collective-permute-start(bf16[16,128,256]{2,1,0:T(8,128)(2,1)} %get-tuple-element.146), channel_id=1, source_target_pairs={{1,25},{3,27},{5,29},{7,31},{33,57},{35,59},{37,61},{39,63},{65,89... | collective-permute-start | bytes 3145736 | tf_op jit(solution)/shard_map/cond/branch_1_fun/ppermute | solution.py:369
  18.8 31.3 %collective-permute-start.11 = (bf16[32,128,256]{2,1,0:T(8,128)(2,1)}, bf16[32,128,256]{2,1,0:T(8,128)(2,1)S(1)}, u32[]{:S(2)}, u32[]{:S(2)}) collective-permute-start(bf16[32,128,256]{2,1,0:T(8,128)(2,1)} %get-tuple-element.151), channel_id=1, source_target_pairs={{1,9},{3,11},{5,13},{7,15},{33,41},{35,43},{37,45},{39,47},{65,73}... | collective-permute-start | bytes 6291464 | tf_op jit(solution)/shard_map/cond/branch_1_fun/ppermute | solution.py:369
  20.2 35.7 %collective-permute-start.12 = (bf16[32,128,256]{2,1,0:T(8,128)(2,1)}, bf16[32,128,256]{2,1,0:T(8,128)(2,1)}, u32[]{:S(2)}, u32[]{:S(2)}) collective-permute-start(bf16[32,128,256]{2,1,0:T(8,128)(2,1)} %get-tuple-element.152), channel_id=1, source_target_pairs={{1,25},{3,27},{5,29},{7,31},{33,57},{35,59},{37,61},{39,63},{65,89... | collective-permute-start | bytes 6291464 | tf_op jit(solution)/shard_map/cond/branch_1_fun/ppermute | solution.py:369
  29.8 18.7 %collective-permute-start.9 = (bf16[16,128,256]{2,1,0:T(8,128)(2,1)}, bf16[16,128,256]{2,1,0:T(8,128)(2,1)S(1)}, u32[]{:S(2)}, u32[]{:S(2)}) collective-permute-start(bf16[16,128,256]{2,1,0:T(8,128)(2,1)} %collective-permute-done.7), channel_id=1, source_target_pairs={{9,17},{11,19},{13,21},{15,23},{41,49},{43,51},{45,53},{47,55},{73... | collective-permute-start | bytes 3145736 | tf_op jit(solution)/shard_map/cond/branch_1_fun/ppermute | solution.py:369
  30.5 18.0 %collective-permute-start.10 = (bf16[16,128,256]{2,1,0:T(8,128)(2,1)}, bf16[16,128,256]{2,1,0:T(8,128)(2,1)}, u32[]{:S(2)}, u32[]{:S(2)}) collective-permute-start(bf16[16,128,256]{2,1,0:T(8,128)(2,1)} %collective-permute-done.8), channel_id=1, source_target_pairs={{25,17},{27,19},{29,21},{31,23},{57,49},{59,51},{61,53},{63,55},{8... | collective-permute-start | bytes 3145736 | tf_op jit(solution)/shard_map/cond/branch_1_fun/ppermute | solution.py:369
  32.2 47.2 %all-to-all-start.1 = ((bf16[256,16,128]{2,1,0:T(8,128)(2,1)}), bf16[256,16,128]{2,1,0:T(8,128)(2,1)}, u32[]{:S(2)}, u32[]{:S(2)}) async-start(bf16[256,16,128]{2,1,0:T(8,128)(2,1)} %branch_1_fun.3), calls=%async_computation.1 | async-start | bytes 2097152 | tf_op jit(solution)/shard_map/cond/branch_1_fun/all_to_all | solution.py:374
  55.9 5.4 %copy-start.1 = (bf16[32,128,256]{2,1,0:T(8,128)(2,1)S(1)}, bf16[32,128,256]{2,1,0:T(8,128)(2,1)}, u32[]{:S(2)}) copy-start(bf16[32,128,256]{2,1,0:T(8,128)(2,1)} %get-tuple-element.153.refs_4_) | copy-start | bytes 6291460 | tf_op jit(solution)/shard_map/cond
  57.8 3.6 %collective-permute-start.13 = (bf16[32,64,256]{2,1,0:T(8,128)(2,1)S(1)}, bf16[32,64,256]{2,1,0:T(8,128)(2,1)S(1)}, u32[]{:S(2)}, u32[]{:S(2)}) collective-permute-start(bf16[32,64,256]{2,1,0:T(8,128)(2,1)S(1)} %branch_1_fun.4), channel_id=1, source_target_pairs={{1,0},{3,2},{5,4},{7,6},{9,8},{11,10},{13,12},{15,14},{17,16},{19,... | collective-permute-start | bytes 3145736 | tf_op jit(solution)/shard_map/cond/branch_1_fun/ppermute | solution.py:379
